TPU v7x, 32 devices: a whole 2x2x4 slice. The times are simulated.
32 devices in a mesh: groups: 2 (over y), seq: 8 (over z, x), wt: 2 (over core).
Axes of the slice: x: 2, y: 2, z: 4, core: 2. Of those that a mesh axis runs over, the one named last changes fastest.
Arguments:
- query_input: bfloat16 [8192, 4096], P(('groups', 'seq'), 'wt'), parts along dimension 0, may hold values from -6 to 6
- key_input: bfloat16 [8192, 4096], P(('groups', 'seq'), 'wt'), parts along dimension 0, may hold values from -6 to 6
- value_input: bfloat16 [8192, 4096], P(('groups', 'seq'), 'wt'), parts along dimension 0, may hold values from -6 to 6
- gate_input: bfloat16 [8192, 4096], P(('groups', 'seq'), 'wt'), parts along dimension 0, may hold values from -6 to 6
- segment: int32 [8192], P(('groups', 'seq')), parts along dimension 0, may hold values from 0 to 7, never falling along the last dimension, each value on 1 to 1024 neighbouring positions
- decay_exponent: int32 [32], P('wt'), may hold values from 5 to 21
- retention: float32 [32, 8192], P('wt', ('groups', 'seq')), parts along dimension 1, may hold values from 0.5 to 1
- norm_gain: float32 [4096], P('wt'), may hold values from 0.5 to 1.5
Outputs:
- gated: bfloat16 [8192, 4096], P(('groups', 'seq'), 'wt'), parts along dimension 0
- snapshots: float32 [16, 32, 128, 128], P(('groups', 'seq'), 'wt'), parts along dimension 0
There are 2 independent parts, one for each index of `groups`. A program takes and returns all parts, laid end to end along the dimension named above; an argument that names none is the same for every part. Nothing has to cross between parts.
Inputs may be any that keep to these rules, and one draw needn't show every extreme that they name: `segment`: never falls along the slab and starts at 0.
All inputs are finite; a program needn't handle non-finite values.
Results may differ from a plain program's by a relative error of at most 0.0047.
Values sent between devices are 32-bit elements; how exact they have to be, the bound alone decides.
No kernel may reach another device: no remote copies, remote signals or barrier semaphores. Data moves between devices by JAX's collectives and lax.ppermute only.
A program may use at most 192 MiB of HBM per device.

v0:
```python
import functools

import jax
import jax.numpy as jnp
from jax import lax
from jax.experimental import pallas as pl
from jax.experimental.pallas import tpu as pltpu
from jax.sharding import PartitionSpec as P

F32 = jnp.float32
BF16 = jnp.bfloat16
NN = (((1,), (0,)), ((), ()))
NT = (((1,), (1,)), ((), ()))
MIB = 1 << 20


def vmem_spec(shape, index_map):
    return pl.BlockSpec(shape, index_map)


def as_column(row, lanes):
    return jnp.broadcast_to(row, (lanes, row.shape[1])).T


def meta_rows(heads):
    return -(-(heads + 1) // 8) * 8


def put_message(msg_ref, first, heads, size, w_ref, finals, end, k_ref, v_ref):
    top = heads * size
    for j in range(heads):
        columns = slice(j * size, (j + 1) * size)
        weight = w_ref[first + j : first + j + 1, :]
        keyed = (k_ref[:, columns].astype(F32).T * weight).astype(BF16)
        msg_ref[columns, :] = lax.dot_general(
            keyed, v_ref[:, columns], NN, preferred_element_type=F32
        )
    msg_ref[top : top + heads, :] = jnp.broadcast_to(finals, (heads, size))
    below = meta_rows(heads) - heads
    msg_ref[top + heads :, :] = jnp.broadcast_to(end.astype(F32), (below, size))


def first_kernel(
    heads,
    chunk,
    order_ref,
    seg_hbm,
    exponent_hbm,
    keep_hbm,
    k_hbm,
    v_hbm,
    msg_ref,
    a_ref,
    w_ref,
    seg_ref,
    k_ref,
    v_ref,
    exponent_ref,
    keep_ref,
    sems,
):
    tokens = seg_ref.shape[1]
    size = msg_ref.shape[1]
    wide = pl.ds(0, chunk * size)
    copies = [
        pltpu.make_async_copy(source, target, sems.at[i])
        for i, (source, target) in enumerate(
            [
                (keep_hbm, keep_ref),
                (exponent_hbm, exponent_ref),
                (seg_hbm, seg_ref),
                (k_hbm.at[:, wide], k_ref),
                (v_hbm.at[:, wide], v_ref),
            ]
        )
    ]
    for copy in copies:
        copy.start()
    earlier = lax.broadcasted_iota(jnp.int32, (tokens, tokens), 0)
    later = lax.broadcasted_iota(jnp.int32, (tokens, tokens), 1)
    upper = jnp.where(earlier <= later, 1.0, 0.0).astype(BF16)
    across = lax.broadcasted_iota(jnp.int32, (heads, heads), 1)
    down = lax.broadcasted_iota(jnp.int32, (heads, heads), 0)
    for copy in copies[:3]:
        copy.wait()
    spread = jnp.broadcast_to(exponent_ref[...], (heads, heads))
    exponent = jnp.sum(jnp.where(across == down, spread, 0).astype(F32), axis=1, keepdims=True)
    a = -jnp.exp2(-exponent) + jnp.log(keep_ref[...])
    high = a.astype(BF16)
    rest = a - high.astype(F32)
    middle = rest.astype(BF16)
    low = (rest - middle.astype(F32)).astype(BF16)
    parts = jnp.concatenate([high, middle, low], axis=0)
    sums = lax.dot_general(parts, upper, NN, preferred_element_type=F32)
    cumulative = sums[:heads] + (sums[heads : 2 * heads] + sums[2 * heads :])
    a_ref[...] = cumulative
    final = cumulative[:, tokens - 1 :]
    seg = seg_ref[...]
    last = seg[:, tokens - 1 :]
    w_ref[...] = jnp.where(seg == last, jnp.exp(final - cumulative), 0.0)
    for copy in copies[3:]:
        copy.wait()
    put_message(msg_ref, 0, chunk, size, w_ref, final[:chunk], last, k_ref, v_ref)


def first_message(order, seg, exponent, keep, k, v, heads, chunk):
    tokens, size = k.shape[0], k.shape[1] // heads
    rows = chunk * size + meta_rows(chunk)
    return pl.pallas_call(
        functools.partial(first_kernel, heads, chunk),
        in_specs=[pl.BlockSpec(memory_space=pltpu.SMEM)]
        + [pl.BlockSpec(memory_space=pltpu.HBM)] * 5,
        out_specs=[pl.BlockSpec(memory_space=pltpu.VMEM)] * 6,
        out_shape=[
            pltpu.VMEM((rows, size), F32),
            pltpu.VMEM((heads, tokens), F32),
            pltpu.VMEM((heads, tokens), F32),
            pltpu.VMEM((1, tokens), jnp.int32),
            pltpu.VMEM((tokens, chunk * size), BF16),
            pltpu.VMEM((tokens, chunk * size), BF16),
        ],
        scratch_shapes=[
            pltpu.VMEM((1, heads), jnp.int32),
            pltpu.VMEM((heads, tokens), F32),
            pltpu.SemaphoreType.DMA((5,)),
        ],
        compiler_params=pltpu.CompilerParams(vmem_limit_bytes=8 * MIB),
        cost_estimate=pl.CostEstimate(
            flops=2 * tokens * chunk * size * size, bytes_accessed=2 * MIB, transcendentals=0
        ),
        name="first_message",
    )(order, seg, exponent, keep, k, v)


def rest_kernel(chunk, seg_ref, a_ref, w_ref, q_hbm, k_hbm, v_hbm, g_hbm, *refs):
    tokens = seg_ref.shape[1]
    count = a_ref.shape[0] // chunk
    messages, refs = refs[: count - 1], refs[count - 1 :]
    mask_ref, refs, sems = refs[0], refs[1:-1], refs[-1]
    k_refs, refs = refs[: count - 1], refs[count - 1 :]
    v_refs, refs = refs[: count - 1], refs[count - 1 :]
    q_refs, g_refs = refs[:count], refs[count:]
    size = messages[0].shape[1]
    pairs = []
    for i in range(1, count):
        wide = pl.ds(i * chunk * size, chunk * size)
        pairs += [(k_hbm.at[:, wide], k_refs[i - 1]), (v_hbm.at[:, wide], v_refs[i - 1])]
    for i in range(count):
        wide = pl.ds(i * chunk * size, chunk * size)
        pairs += [(q_hbm.at[:, wide], q_refs[i]), (g_hbm.at[:, wide], g_refs[i])]
    copies = [pltpu.make_async_copy(*pair, sems.at[i]) for i, pair in enumerate(pairs)]
    for copy in copies:
        copy.start()
    make_mask(seg_ref, mask_ref)
    last = seg_ref[:, tokens - 1 :]
    for i, msg_ref in enumerate(messages):
        copies[2 * i].wait()
        copies[2 * i + 1].wait()
        first = (i + 1) * chunk
        final = a_ref[first : first + chunk, tokens - 1 :]
        put_message(msg_ref, first, chunk, size, w_ref, final, last, k_refs[i], v_refs[i])
    for copy in copies[2 * len(messages) :]:
        copy.wait()


def rest_messages(seg, a, w, q, k, v, g, chunk):
    heads = a.shape[0]
    tokens, size = k.shape[0], k.shape[1] // heads
    count = heads // chunk
    rows = chunk * size + meta_rows(chunk)
    arrays = 4 * count - 2
    out = pl.pallas_call(
        functools.partial(rest_kernel, chunk),
        in_specs=[pl.BlockSpec(memory_space=pltpu.VMEM)] * 3
        + [pl.BlockSpec(memory_space=pltpu.HBM)] * 4,
        out_specs=[pl.BlockSpec(memory_space=pltpu.VMEM)] * (count + arrays),
        out_shape=[pltpu.VMEM((rows, size), F32)] * (count - 1)
        + [pltpu.VMEM((tokens, tokens), F32)]
        + [pltpu.VMEM((tokens, chunk * size), BF16)] * arrays,
        scratch_shapes=[pltpu.SemaphoreType.DMA((arrays,))],
        compiler_params=pltpu.CompilerParams(vmem_limit_bytes=8 * MIB),
        cost_estimate=pl.CostEstimate(
            flops=2 * tokens * heads * size * size, bytes_accessed=8 * MIB, transcendentals=0
        ),
        name="rest_messages",
    )(seg, a, w, q, k, v, g)
    messages, mask, out = out[: count - 1], out[count - 1], out[count:]
    k_near, out = out[: count - 1], out[count - 1 :]
    v_near, out = out[: count - 1], out[count - 1 :]
    return messages, mask, k_near, v_near, out[:count], out[count:]


def join_kernel(heads, order_ref, mine_ref, other_ref, *rest):
    *copied, out_ref = rest
    if copied:
        copied[-1][...] = copied[0][...]
    size = mine_ref.shape[1]
    top = heads * size
    mine_later = (order_ref[0] & 1) == 1
    final_mine, final_other = mine_ref[top : top + heads, :], other_ref[top : top + heads, :]
    end_mine, end_other = mine_ref[top + heads :, :], other_ref[top + heads :, :]
    same = jnp.where(end_mine[:1] == end_other[:1], 1.0, 0.0)
    scale_mine = jnp.where(mine_later, 1.0, jnp.exp(final_other) * same)
    scale_other = jnp.where(mine_later, jnp.exp(final_mine) * same, 1.0)
    for head in range(heads):
        rows = slice(head * size, (head + 1) * size)
        out_ref[rows, :] = (
            scale_mine[head : head + 1] * mine_ref[rows, :]
            + scale_other[head : head + 1] * other_ref[rows, :]
        )
    out_ref[top : top + heads, :] = final_mine + final_other
    out_ref[top + heads :, :] = jnp.where(mine_later, end_mine, end_other)


def joined(order, mine, other, heads, after=(), through=()):
    rows, size = mine.shape
    message = pltpu.VMEM((rows, size), F32)
    vmem, anywhere = pl.BlockSpec(memory_space=pltpu.VMEM), pl.BlockSpec(memory_space=pl.ANY)

    def kernel(order_ref, mine_ref, other_ref, *rest):
        rest = rest[: len(through)] + rest[len(through) + len(after) :]
        join_kernel(heads, order_ref, mine_ref, other_ref, *rest)

    return pl.pallas_call(
        kernel,
        in_specs=[pl.BlockSpec(memory_space=pltpu.SMEM), vmem, vmem]
        + [vmem] * len(through)
        + [anywhere] * len(after),
        out_specs=[vmem] * (len(through) + 1),
        out_shape=[message] * (len(through) + 1),
        compiler_params=pltpu.CompilerParams(vmem_limit_bytes=8 * MIB),
        cost_estimate=pl.CostEstimate(
            flops=3 * rows * size, bytes_accessed=12 * rows * size, transcendentals=0
        ),
        name="join_windows",
    )(order, mine, other, *through, *after)


def make_mask(seg_ref, mask_ref):
    tokens = seg_ref.shape[1]
    seg = seg_ref[...].astype(F32)
    column = as_column(seg, 128)
    for start in range(0, tokens, 128):
        across = lax.broadcasted_iota(jnp.int32, (tokens, 128), 1) + start
        down = lax.broadcasted_iota(jnp.int32, (tokens, 128), 0)
        seen = (column == seg[:, start : start + 128]) & (across <= down)
        mask_ref[:, start : start + 128] = jnp.where(seen, 0.0, -1e30)


def intra_kernel(
    first, heads, mask_ref, a_ref, gain_ref, q_ref, k_ref, v_ref, g_ref, o_ref, gate_ref
):
    tokens = mask_ref.shape[0]
    size = q_ref.shape[1] // heads
    block = min(tokens, 256)
    for j in range(heads):
        columns = slice(j * size, (j + 1) * size)
        a_row = a_ref[first + j : first + j + 1, :] * 1.4426950408889634
        a_column = as_column(a_row, 128)
        for start in range(0, tokens, block):
            here, upto = slice(start, start + block), slice(0, start + block)
            scores = lax.dot_general(
                q_ref[here, columns], k_ref[upto, columns], NT, preferred_element_type=F32
            )
            spread = jnp.concatenate([a_column[here]] * ((start + block) // 128), axis=1)
            weight = jnp.exp2(spread - a_row[:, upto] + mask_ref[here, upto])
            probs = (scores * weight).astype(BF16)
            o_ref[here, columns] = lax.dot_general(
                probs, v_ref[upto, columns], NN, preferred_element_type=F32
            )
        half = 0.5 * gain_ref[:, (first + j) * size : (first + j + 1) * size]
        gate_ref[:, columns] = half + half * jnp.tanh(0.5 * g_ref[:, columns].astype(F32))


def intra(mask, a, gain, q, k, v, g, first, heads):
    tokens, size = mask.shape[0], gain.shape[1] // a.shape[0]
    vmem = pl.BlockSpec(memory_space=pltpu.VMEM)
    o, gate = pl.pallas_call(
        functools.partial(intra_kernel, first, heads),
        in_specs=[vmem] * 7,
        out_specs=[vmem] * 2,
        out_shape=[pltpu.VMEM((tokens, heads * size), F32)] * 2,
        compiler_params=pltpu.CompilerParams(vmem_limit_bytes=8 * MIB),
        cost_estimate=pl.CostEstimate(
            flops=3 * tokens * tokens * heads * size,
            bytes_accessed=3 * MIB,
            transcendentals=tokens * tokens * heads,
        ),
        name="intra_span",
    )(mask, a, gain, q, k, v, g)
    return o, gate, q


def final_kernel(
    first,
    heads,
    order_ref,
    seg_ref,
    own_ref,
    pair_ref,
    before_ref,
    o_ref,
    gate_ref,
    q_ref,
    a_ref,
    *rest,
):
    rest = rest[2 * (first > 0) :]
    gated_hbm, snap_hbm, gated_ref, snap_ref, sems = rest[:2] + rest[-3:]
    if first == 0:
        rest[2][...] = jnp.zeros_like(rest[2])
    tokens, size = q_ref.shape[0], own_ref.shape[1]
    block = min(tokens, 256)
    top = heads * size
    second = (order_ref[0] & 1) == 1
    ends = slice(top + heads, top + heads + 1)
    finals = slice(top, top + heads)
    own_end, pair_end, before_end = own_ref[ends, :], pair_ref[ends, :], before_ref[ends, :]
    previous = jnp.where(second, pair_end, before_end)
    kept = jnp.where(own_end == previous, 1.0, 0.0)
    bridged = jnp.where(pair_end == before_end, 1.0, 0.0)
    own_decay = jnp.exp(own_ref[finals, :]) * kept
    from_before = jnp.where(second, jnp.exp(pair_ref[finals, :]) * bridged, 1.0)
    from_before = jnp.where(order_ref[0] >= 2, from_before, 0.0)
    from_pair = jnp.where(second, 1.0, 0.0)
    valid = seg_ref[...].astype(F32) == previous[:, :1]
    copies = []
    for j in range(heads):
        rows = columns = slice(j * size, (j + 1) * size)
        state = from_before[j : j + 1] * before_ref[rows, :] + from_pair * pair_ref[rows, :]
        snap_ref[j] = own_decay[j : j + 1] * state + own_ref[rows, :]
        high = state.astype(BF16)
        low = (state - high.astype(F32)).astype(BF16)
        q = q_ref[:, columns]
        both = jnp.concatenate([high, low], axis=0)
        decay = jnp.where(valid, jnp.exp(a_ref[first + j : first + j + 1, :]), 0.0)
        decay = as_column(decay, size)
        for start in range(0, tokens, block):
            here = slice(start, start + block)
            inter = lax.dot_general(
                jnp.concatenate([q[here], q[here]], axis=1), both, NN, preferred_element_type=F32
            )
            mixed = o_ref[here, columns] + inter * decay[here]
            mean_square = jnp.mean(mixed * mixed, axis=1, keepdims=True)
            gated = mixed * lax.rsqrt(mean_square + 1e-06) * gate_ref[here, columns]
            gated_ref[here, columns] = gated.astype(BF16)
        if j % 2 == 1 or j == heads - 1:
            begin = j - j % 2
            width = (j + 1 - begin) * size
            heads_here = pl.ds(first + begin, j + 1 - begin)
            place = pl.ds((first + begin) * size, width)
            for source, target in (
                (gated_ref.at[:, pl.ds(begin * size, width)], gated_hbm.at[:, place]),
                (snap_ref.at[pl.ds(begin, j + 1 - begin)], snap_hbm.at[0, heads_here]),
            ):
                copies.append(pltpu.make_async_copy(source, target, sems.at[len(copies)]))
                copies[-1].start()
    for copy in copies:
        copy.wait()


def finish(order, seg, own, pair, before, o, gate, q, a, so_far, first, heads):
    tokens, size = q.shape[0], q.shape[1] // heads
    total = a.shape[0]
    vmem, anywhere = pl.BlockSpec(memory_space=pltpu.VMEM), pl.BlockSpec(memory_space=pl.ANY)
    return pl.pallas_call(
        functools.partial(final_kernel, first, heads),
        in_specs=[pl.BlockSpec(memory_space=pltpu.SMEM)] + [vmem] * 8 + [anywhere] * len(so_far),
        out_specs=[anywhere, anywhere] + [vmem] * (first == 0),
        out_shape=[
            jax.ShapeDtypeStruct((tokens, total * size), BF16),
            jax.ShapeDtypeStruct((1, total, size, size), F32),
        ]
        + [pltpu.VMEM((8, 128), F32)] * (first == 0),
        scratch_shapes=[
            pltpu.VMEM((tokens, heads * size), BF16),
            pltpu.VMEM((heads, size, size), F32),
            pltpu.SemaphoreType.DMA((2 * heads,)),
        ],
        input_output_aliases={9 + i: i for i in range(len(so_far))},
        compiler_params=pltpu.CompilerParams(vmem_limit_bytes=8 * MIB),
        cost_estimate=pl.CostEstimate(
            flops=4 * tokens * heads * size * size,
            bytes_accessed=4 * MIB,
            transcendentals=2 * tokens * heads * size,
        ),
        name="finish",
    )(order, seg, own, pair, before, o, gate, q, a, *so_far)


def shards(q, k, v, g, segment, decay_exponent, retention, norm_gain):
    heads = decay_exponent.shape[0]
    tokens = q.shape[0]
    count = lax.axis_size("seq")
    place = lax.axis_index("seq")
    reach = max(1, count // 4)
    chunk = 4
    firsts = list(range(0, heads, chunk))
    last = len(firsts) - 1
    far = lambda x: pltpu.with_memory_space_constraint(x, pltpu.HBM)
    q, k, v, g = far(q), far(k), far(v), far(g)
    gain = norm_gain.reshape(1, -1)
    order = jnp.where(place >= 2, 2 + (place & 1), place & 1).astype(jnp.int32).reshape(1)
    swap = [(c, c ^ 1) for c in range(count)]
    turn = [(c, (c + 2) % count) for c in range(count)]

    pair, before, inside = {}, {}, {}
    result = ()

    own0, a, w, seg, k0, v0 = first_message(
        order,
        far(segment.reshape(1, tokens)),
        far(decay_exponent.reshape(1, heads)),
        far(retention),
        k,
        v,
        heads,
        chunk,
    )
    own = [own0]
    pair[0] = lax.ppermute(own[0], "seq", swap)
    messages, mask, k_near, v_near, q_near, g_near = rest_messages(seg, a, w, q, k, v, g, chunk)
    own += messages
    k_near, v_near = [k0, *k_near], [v0, *v_near]
    pair[1] = lax.ppermute(own[1], "seq", swap)

    for i, first in enumerate(firsts):
        inside[i] = intra(
            mask, a, gain, q_near[i], k_near[i], v_near[i], g_near[i], first, chunk
        )
        after = (inside[i][0],) + ((done,) if i == last else ())
        through = (own[i + 2],) if i + 2 <= last else ()
        *through, both = joined(order, own[i], pair[i], chunk, after, through)
        if through:
            own[i + 2] = through[0]
            pair[i + 2] = lax.ppermute(own[i + 2], "seq", swap)
        before[i] = lax.ppermute(both, "seq", turn)
        window = 2
        if window < reach:
            before[i] = jnp.where(place >= 2, before[i], 0.0)
        while window < reach:
            past = lax.ppermute(before[i], "seq", [(c, c + window) for c in range(count - window)])
            (before[i],) = joined(jnp.ones((1,), jnp.int32), before[i], past, chunk)
            window *= 2
        for j in {last - 1: (0,), last: range(1, last + 1)}.get(i, ()):
            result = finish(
                order, seg, own[j], pair[j], before[j], *inside[j], a, result, firsts[j], chunk
            )
            if j == 0:
                *result, done = result
    return tuple(result)


def solution(mesh):
    placed = (
        P(("groups", "seq"), "wt"),
        P(("groups", "seq"), "wt"),
        P(("groups", "seq"), "wt"),
        P(("groups", "seq"), "wt"),
        P(("groups", "seq")),
        P("wt"),
        P("wt", ("groups", "seq")),
        P("wt"),
    )
    return jax.shard_map(
        shards,
        mesh=mesh,
        in_specs=placed,
        out_specs=(P(("groups", "seq"), "wt"), P(("groups", "seq"), "wt", None, None)),
        check_vma=False,
    )
```

profile of v0, /device:TPU:0, one launch (start us, length us, event | category | flops | bytes accessed | tf_op | source)
XLA Modules:
  0.0 42.9 jit_solution(14093916127389495438)
XLA Ops:
  0.6 1.7 %first_message.1 = (f32[520,128]{1,0:T(8,128)S(1)}, f32[16,512]{1,0:T(8,128)S(1)}, f32[16,512]{1,0:T(8,128)S(1)}, s32[1,512]{1,0:T(1,128)S(1)}, bf16[512,512]{1,...) custom-call(s32[1]{0:T(128)} %bitcast.order_ref, s32[1,512]{1,0:T(1,128)} %bitcast.8, s32[1,16]{1,0:T(1,128)} %bitcast.9, ...), custom_call_target="tpu_custom_call" | custom-call | flops 67108864 | bytes 2097152 | tf_op jit(solution)/shard_map/first_message/pallas_call | solution.py:109
  2.3 3.0 %collective-permute-start.2 = (f32[520,128]{1,0:T(8,128)S(1)}, f32[520,128]{1,0:T(8,128)S(1)}, u32[]{:S(2)}, u32[]{:S(2)}) collective-permute-start(f32[520,128]{1,0:T(8,128)S(1)} %get-tuple-element.62.mine_ref.own_ref), channel_id=1, source_target_pairs={{0,2},{2,0},{4,6},{6,4},{8,10},{10,8},{12,14},{14,12},{1,3},{3,1},... | collective-permute-start | bytes 798728 | tf_op jit(solution)/shard_map/ppermute | solution.py:421
  5.3 3.3 %rest_messages.1 = (f32[520,128]{1,0:T(8,128)S(1)}, f32[520,128]{1,0:T(8,128)S(1)}, f32[520,128]{1,0:T(8,128)S(1)}, f32[512,512]{1,0:T(8,128)S(1)}, bf16[512,512...) custom-call(s32[1,512]{1,0:T(1,128)S(1)} %get-tuple-element.45.seg_r, ...), custom_call_target="tpu_custom_call" | custom-call | flops 268435456 | bytes 8388608 | tf_op jit(solution)/shard_map/rest_messages/pallas_call | solution.py:172
  8.6 0.1 collective-permute-start
  8.7 1.5 %intra_span.6 = (f32[512,512]{1,0:T(8,128)S(1)}, f32[512,512]{1,0:T(8,128)S(1)}) custom-call(f32[512,512]{1,0:T(8,128)S(1)} %get-tuple-element.50.mask_ref, f32[16,512]{1,0:T(8,128)S(1)} %get-tuple-element.46.a_ref, f32[1,2048]{1,0:T(1,128)S(1)} %bitcast.4, bf16[512,512]{1,0:T(8,128)(2,1)S(1)} %get-tuple-element.64.q_ref, ...), custom_call_target="tpu_custom_call" | custom-call | flops 402653184 | bytes 3145728 | tf_op jit(solution)/shard_map/intra_span/pallas_call | solution.py:278
  10.2 2.3 %collective-permute-done.2.other_ref.pair_ref = f32[520,128]{1,0:T(8,128)S(1)} collective-permute-done((f32[520,128]{1,0:T(8,128)S(1)}, f32[520,128]{1,0:T(8,128)S(1)}, u32[]{:S(2)}, u32[]{:S(2)}) %collective-permute-start.2) | collective-permute-done | bytes 266272 | tf_op jit(solution)/shard_map/ppermute | solution.py:421
  12.6 2.1 %collective-permute-start.3 = (f32[520,128]{1,0:T(8,128)S(1)}, f32[520,128]{1,0:T(8,128)S(1)}, u32[]{:S(2)}, u32[]{:S(2)}) collective-permute-start(f32[520,128]{1,0:T(8,128)S(1)} %get-tuple-element.69), channel_id=1, source_target_pairs={{0,4},{2,6},{4,8},{6,10},{8,12},{10,14},{12,0},{14,2},{1,5},{3,7},... | collective-permute-start | bytes 798728 | tf_op jit(solution)/shard_map/ppermute | solution.py:437
  14.7 1.6 %collective-permute-start.5 = (f32[520,128]{1,0:T(8,128)S(1)}, f32[520,128]{1,0:T(8,128)S(1)}, u32[]{:S(2)}, u32[]{:S(2)}) collective-permute-start(f32[520,128]{1,0:T(8,128)S(1)} %get-tuple-element.73.mine_ref.own_ref), channel_id=1, source_target_pairs={{0,2},{2,0},{4,6},{6,4},{8,10},{10,8},{12,14},{14,12},{1,3},{3,1},... | collective-permute-start | bytes 798728 | tf_op jit(solution)/shard_map/ppermute | solution.py:436
  16.3 1.5 %intra_span.4 = (f32[512,512]{1,0:T(8,128)S(1)}, f32[512,512]{1,0:T(8,128)S(1)}) custom-call(f32[512,512]{1,0:T(8,128)S(1)} %get-tuple-element.50.mask_ref, f32[16,512]{1,0:T(8,128)S(1)} %get-tuple-element.46.a_ref, f32[1,2048]{1,0:T(1,128)S(1)} %bitcast.5, bf16[512,512]{1,0:T(8,128)(2,1)S(1)} %get-tuple-element.51.q_ref, ...), custom_call_target="tpu_custom_call" | custom-call | flops 402653184 | bytes 3145728 | tf_op jit(solution)/shard_map/intra_span/pallas_call | solution.py:278
  17.8 0.4 %collective-permute-done.other_ref.pair_ref = f32[520,128]{1,0:T(8,128)S(1)} collective-permute-done((f32[520,128]{1,0:T(8,128)S(1)}, f32[520,128]{1,0:T(8,128)S(1)}, u32[]{:S(2)}, u32[]{:S(2)}) %collective-permute-start) | collective-permute-done | bytes 266272 | tf_op jit(solution)/shard_map/ppermute | solution.py:425
  18.3 2.1 %collective-permute-start.1 = (f32[520,128]{1,0:T(8,128)S(1)}, f32[520,128]{1,0:T(8,128)S(1)}, u32[]{:S(2)}, u32[]{:S(2)}) collective-permute-start(f32[520,128]{1,0:T(8,128)S(1)} %get-tuple-element.56.mine_ref.own_ref), channel_id=1, source_target_pairs={{0,2},{2,0},{4,6},{6,4},{8,10},{10,8},{12,14},{14,12},{1,3},{3,1},... | collective-permute-start | bytes 798728 | tf_op jit(solution)/shard_map/ppermute | solution.py:436
  20.4 1.5 %intra_span.7 = (f32[512,512]{1,0:T(8,128)S(1)}, f32[512,512]{1,0:T(8,128)S(1)}) custom-call(f32[512,512]{1,0:T(8,128)S(1)} %get-tuple-element.50.mask_ref, f32[16,512]{1,0:T(8,128)S(1)} %get-tuple-element.46.a_ref, f32[1,2048]{1,0:T(1,128)S(1)} %bitcast.6, bf16[512,512]{1,0:T(8,128)(2,1)S(1)} %get-tuple-element.74.q_ref, ...), custom_call_target="tpu_custom_call" | custom-call | flops 402653184 | bytes 3145728 | tf_op jit(solution)/shard_map/intra_span/pallas_call | solution.py:278
  22.0 1.6 %collective-permute-start.7 = (f32[520,128]{1,0:T(8,128)S(1)}, f32[520,128]{1,0:T(8,128)S(1)}, u32[]{:S(2)}, u32[]{:S(2)}) collective-permute-start(f32[520,128]{1,0:T(8,128)S(1)} %get-tuple-element.80), channel_id=1, source_target_pairs={{0,4},{2,6},{4,8},{6,10},{8,12},{10,14},{12,0},{14,2},{1,5},{3,7},... | collective-permute-start | bytes 798728 | tf_op jit(solution)/shard_map/ppermute | solution.py:437
  23.6 1.5 %intra_span.5 = (f32[512,512]{1,0:T(8,128)S(1)}, f32[512,512]{1,0:T(8,128)S(1)}) custom-call(f32[512,512]{1,0:T(8,128)S(1)} %get-tuple-element.50.mask_ref, f32[16,512]{1,0:T(8,128)S(1)} %get-tuple-element.46.a_ref, f32[1,2048]{1,0:T(1,128)S(1)} %bitcast.7, bf16[512,512]{1,0:T(8,128)(2,1)S(1)} %get-tuple-element.57.q_ref, ...), custom_call_target="tpu_custom_call" | custom-call | flops 402653184 | bytes 3145728 | tf_op jit(solution)/shard_map/intra_span/pallas_call | solution.py:278
  25.2 1.6 %collective-permute-start.6 = (f32[520,128]{1,0:T(8,128)S(1)}, f32[520,128]{1,0:T(8,128)S(1)}, u32[]{:S(2)}, u32[]{:S(2)}) collective-permute-start(f32[520,128]{1,0:T(8,128)S(1)} %join_windows.7), channel_id=1, source_target_pairs={{0,4},{2,6},{4,8},{6,10},{8,12},{10,14},{12,0},{14,2},{1,5},{3,7},... | collective-permute-start | bytes 798728 | tf_op jit(solution)/shard_map/ppermute | solution.py:437
  26.8 1.7 %finish.4 = (bf16[512,2048]{1,0:T(8,128)(2,1)}, f32[1,16,128,128]{3,2,1,0:T(8,128)}, f32[8,128]{1,0:T(8,128)S(1)}) custom-call(s32[1]{0:T(128)} %bitcast.order_ref, s32[1,512]{1,0:T(1,128)S(1)} %get-tuple-element.45.seg_ref, f32[520,128]{1,0:T(8,128)S(1)} %get-tuple-element.62.mine_ref.own_ref, f32[520,128]{1,0:T(8,128)S(1)} %collective-permute-done.2.other_ref.pair_ref, ...), custom_call_target="tpu_custom_call" | custom-call | flops 134217728 | bytes 4194304 | tf_op jit(solution)/shard_map/finish/pallas_call | solution.py:366
  28.5 0.3 collective-permute-done.1.other_ref.pair_ref
  28.9 1.9 %collective-permute-start.4 = (f32[520,128]{1,0:T(8,128)S(1)}, f32[520,128]{1,0:T(8,128)S(1)}, u32[]{:S(2)}, u32[]{:S(2)}) collective-permute-start(f32[520,128]{1,0:T(8,128)S(1)} %join_windows.6), channel_id=1, source_target_pairs={{0,4},{2,6},{4,8},{6,10},{8,12},{10,14},{12,0},{14,2},{1,5},{3,7},... | collective-permute-start | bytes 798728 | tf_op jit(solution)/shard_map/ppermute | solution.py:437
  30.8 1.9 %collective-permute-done.7.before_ref = f32[520,128]{1,0:T(8,128)S(1)} collective-permute-done((f32[520,128]{1,0:T(8,128)S(1)}, f32[520,128]{1,0:T(8,128)S(1)}, u32[]{:S(2)}, u32[]{:S(2)}) %collective-permute-start.7) | collective-permute-done | bytes 266272 | tf_op jit(solution)/shard_map/ppermute | solution.py:437
  32.7 1.7 %finish.5 = (bf16[512,2048]{1,0:T(8,128)(2,1)}, f32[1,16,128,128]{3,2,1,0:T(8,128)}) custom-call(s32[1]{0:T(128)} %bitcast.order_ref, s32[1,512]{1,0:T(1,128)S(1)} %get-tuple-element.45.seg_ref, f32[520,128]{1,0:T(8,128)S(1)} %get-tuple-element.48.mine_ref.own_ref, ...), custom_call_target="tpu_custom_call", output_to_operand_aliasing={{0}: (9, {}), {1}: (10, {})} | custom-call | flops 134217728 | bytes 4194304 | tf_op jit(solution)/shard_map/finish/pallas_call | solution.py:366
  34.4 4.0 %collective-permute-done.6.before_ref = f32[520,128]{1,0:T(8,128)S(1)} collective-permute-done((f32[520,128]{1,0:T(8,128)S(1)}, f32[520,128]{1,0:T(8,128)S(1)}, u32[]{:S(2)}, u32[]{:S(2)}) %collective-permute-start.6) | collective-permute-done | bytes 266272 | tf_op jit(solution)/shard_map/ppermute | solution.py:437
  38.4 1.6 %finish.6 = (bf16[512,2048]{1,0:T(8,128)(2,1)}, f32[1,16,128,128]{3,2,1,0:T(8,128)}) custom-call(s32[1]{0:T(128)} %bitcast.order_ref, s32[1,512]{1,0:T(1,128)S(1)} %get-tuple-element.45.seg_ref, f32[520,128]{1,0:T(8,128)S(1)} %get-tuple-element.73.mine_ref.own_ref, ...), custom_call_target="tpu_custom_call", output_to_operand_aliasing={{0}: (9, {}), {1}: (10, {})} | custom-call | flops 134217728 | bytes 4194304 | tf_op jit(solution)/shard_map/finish/pallas_call | solution.py:366
  40.0 1.3 %collective-permute-done.4.before_ref = f32[520,128]{1,0:T(8,128)S(1)} collective-permute-done((f32[520,128]{1,0:T(8,128)S(1)}, f32[520,128]{1,0:T(8,128)S(1)}, u32[]{:S(2)}, u32[]{:S(2)}) %collective-permute-start.4) | collective-permute-done | bytes 266272 | tf_op jit(solution)/shard_map/ppermute | solution.py:437
  41.3 1.7 %finish.7 = (bf16[512,2048]{1,0:T(8,128)(2,1)}, f32[1,16,128,128]{3,2,1,0:T(8,128)}) custom-call(s32[1]{0:T(128)} %bitcast.order_ref, s32[1,512]{1,0:T(1,128)S(1)} %get-tuple-element.45.seg_ref, f32[520,128]{1,0:T(8,128)S(1)} %get-tuple-element.56.mine_ref.own_ref, ...), custom_call_target="tpu_custom_call", output_to_operand_aliasing={{0}: (9, {}), {1}: (10, {})} | custom-call | flops 134217728 | bytes 4194304 | tf_op jit(solution)/shard_map/finish/pallas_call | solution.py:366
  (8 shorter events, 0.2 us)
Async XLA Ops:
  2.3 10.2 %collective-permute-start.2 = (f32[520,128]{1,0:T(8,128)S(1)}, f32[520,128]{1,0:T(8,128)S(1)}, u32[]{:S(2)}, u32[]{:S(2)}) collective-permute-start(f32[520,128]{1,0:T(8,128)S(1)} %get-tuple-element.62.mine_ref.own_ref), channel_id=1, source_target_pairs={{0,2},{2,0},{4,6},{6,4},{8,10},{10,8},{12,14},{14,12},{1,3},{3,1},... | collective-permute-start | bytes 798728 | tf_op jit(solution)/shard_map/ppermute | solution.py:421
  5.3 3.4 %copy-start = (f32[2048]{0:T(1024)S(1)}, f32[2048]{0:T(1024)}, u32[]{:S(2)}) copy-start(f32[2048]{0:T(1024)} %param.15) | copy-start | bytes 24580
  8.6 9.6 %collective-permute-start = (f32[520,128]{1,0:T(8,128)S(1)}, f32[520,128]{1,0:T(8,128)S(1)}, u32[]{:S(2)}, u32[]{:S(2)}) collective-permute-start(f32[520,128]{1,0:T(8,128)S(1)} %get-tuple-element.48.mine_ref.own_ref), channel_id=1, source_target_pairs={{0,2},{2,0},{4,6},{6,4},{8,10},{10,8},{12,14},{14,12},{1,3},{3,1},... | collective-permute-start | bytes 798728 | tf_op jit(solution)/shard_map/ppermute | solution.py:425
  12.6 14.2 %collective-permute-start.3 = (f32[520,128]{1,0:T(8,128)S(1)}, f32[520,128]{1,0:T(8,128)S(1)}, u32[]{:S(2)}, u32[]{:S(2)}) collective-permute-start(f32[520,128]{1,0:T(8,128)S(1)} %get-tuple-element.69), channel_id=1, source_target_pairs={{0,4},{2,6},{4,8},{6,10},{8,12},{10,14},{12,0},{14,2},{1,5},{3,7},... | collective-permute-start | bytes 798728 | tf_op jit(solution)/shard_map/ppermute | solution.py:437
  14.7 10.4 %collective-permute-start.5 = (f32[520,128]{1,0:T(8,128)S(1)}, f32[520,128]{1,0:T(8,128)S(1)}, u32[]{:S(2)}, u32[]{:S(2)}) collective-permute-start(f32[520,128]{1,0:T(8,128)S(1)} %get-tuple-element.73.mine_ref.own_ref), channel_id=1, source_target_pairs={{0,2},{2,0},{4,6},{6,4},{8,10},{10,8},{12,14},{14,12},{1,3},{3,1},... | collective-permute-start | bytes 798728 | tf_op jit(solution)/shard_map/ppermute | solution.py:436
  18.3 10.5 %collective-permute-start.1 = (f32[520,128]{1,0:T(8,128)S(1)}, f32[520,128]{1,0:T(8,128)S(1)}, u32[]{:S(2)}, u32[]{:S(2)}) collective-permute-start(f32[520,128]{1,0:T(8,128)S(1)} %get-tuple-element.56.mine_ref.own_ref), channel_id=1, source_target_pairs={{0,2},{2,0},{4,6},{6,4},{8,10},{10,8},{12,14},{14,12},{1,3},{3,1},... | collective-permute-start | bytes 798728 | tf_op jit(solution)/shard_map/ppermute | solution.py:436
  22.0 10.7 %collective-permute-start.7 = (f32[520,128]{1,0:T(8,128)S(1)}, f32[520,128]{1,0:T(8,128)S(1)}, u32[]{:S(2)}, u32[]{:S(2)}) collective-permute-start(f32[520,128]{1,0:T(8,128)S(1)} %get-tuple-element.80), channel_id=1, source_target_pairs={{0,4},{2,6},{4,8},{6,10},{8,12},{10,14},{12,0},{14,2},{1,5},{3,7},... | collective-permute-start | bytes 798728 | tf_op jit(solution)/shard_map/ppermute | solution.py:437
  25.2 13.2 %collective-permute-start.6 = (f32[520,128]{1,0:T(8,128)S(1)}, f32[520,128]{1,0:T(8,128)S(1)}, u32[]{:S(2)}, u32[]{:S(2)}) collective-permute-start(f32[520,128]{1,0:T(8,128)S(1)} %join_windows.7), channel_id=1, source_target_pairs={{0,4},{2,6},{4,8},{6,10},{8,12},{10,14},{12,0},{14,2},{1,5},{3,7},... | collective-permute-start | bytes 798728 | tf_op jit(solution)/shard_map/ppermute | solution.py:437
  28.9 12.4 %collective-permute-start.4 = (f32[520,128]{1,0:T(8,128)S(1)}, f32[520,128]{1,0:T(8,128)S(1)}, u32[]{:S(2)}, u32[]{:S(2)}) collective-permute-start(f32[520,128]{1,0:T(8,128)S(1)} %join_windows.6), channel_id=1, source_target_pairs={{0,4},{2,6},{4,8},{6,10},{8,12},{10,14},{12,0},{14,2},{1,5},{3,7},... | collective-permute-start | bytes 798728 | tf_op jit(solution)/shard_map/ppermute | solution.py:437
where the time goes:
time: 43.1 us; the launch traced here: 42.9 us
  Pallas kernels  17.9 us (42%)
  starting transfers between devices  14 us (32%)
  waiting for transfers between devices  10.3 us (24%)
  between operations  0.73 us (2%)
    ppermute x4, starting transfers between devices, shards(): before[i] = lax.ppermute(both, 'seq', turn)  7.24 us
    ppermute x4, waiting for transfers between devices, shards(): before[i] = lax.ppermute(both, 'seq', turn)  7.21 us
    pallas_call x4, Pallas kernels, finish(): pl.pallas_call(functools.partial(final_kernel, first, heads), in_specs=[p...  6.6 us
    pallas_call x4, Pallas kernels, intra(): pl.pallas_call(functools.partial(intra_kernel, first, heads), in_specs=[v...  6.06 us
    ppermute x2, starting transfers between devices, shards(): pair[i + 2] = lax.ppermute(own[i + 2], 'seq', swap)  3.71 us
    pallas_call x1, Pallas kernels, rest_messages(): pl.pallas_call(functools.partial(rest_kernel, chunk), in_specs=[pl.BlockS...  3.3 us
    ppermute x1, starting transfers between devices, shards(): pair[0] = lax.ppermute(own[0], 'seq', swap)  3 us
    ppermute x1, waiting for transfers between devices, shards(): pair[0] = lax.ppermute(own[0], 'seq', swap)  2.29 us
  transfers between devices with their start and end apart: 8, of which 6 were waited for; matrix products, arithmetic and copies ran while one was open for 0% of the time, Pallas kernels for 34%

commit v1 on v0

v1 whole, which is shorter than its diff:
```python
import functools

import jax
import jax.numpy as jnp
from jax import lax
from jax.experimental import pallas as pl
from jax.experimental.pallas import tpu as pltpu
from jax.sharding import PartitionSpec as P

F32 = jnp.float32
BF16 = jnp.bfloat16
NN = (((1,), (0,)), ((), ()))
NT = (((1,), (1,)), ((), ()))
MIB = 1 << 20
SHORT = pl.CostEstimate(flops=1, bytes_accessed=1, transcendentals=0)


def vmem_spec(shape, index_map):
    return pl.BlockSpec(shape, index_map)


def as_column(row, lanes):
    return jnp.broadcast_to(row, (lanes, row.shape[1])).T


def meta_rows(heads):
    return -(-(heads + 1) // 8) * 8


def put_message(msg_ref, first, heads, size, w_ref, finals, end, k_ref, v_ref):
    top = heads * size
    for j in range(heads):
        columns = slice(j * size, (j + 1) * size)
        weight = w_ref[first + j : first + j + 1, :]
        keyed = (k_ref[:, columns].astype(F32).T * weight).astype(BF16)
        msg_ref[columns, :] = lax.dot_general(
            keyed, v_ref[:, columns], NN, preferred_element_type=F32
        )
    msg_ref[top : top + heads, :] = jnp.broadcast_to(finals, (heads, size))
    below = meta_rows(heads) - heads
    msg_ref[top + heads :, :] = jnp.broadcast_to(end.astype(F32), (below, size))


def first_kernel(heads, chunks, order_ref, seg_hbm, exponent_hbm, keep_hbm, k_hbm, v_hbm, *refs):
    number = len(chunks)
    messages, refs = refs[:number], refs[number:]
    (a_ref, w_ref, seg_ref), refs = refs[:3], refs[3:]
    k_refs, v_refs, refs = refs[:number], refs[number : 2 * number], refs[2 * number :]
    exponent_ref, keep_ref, sems = refs
    tokens = seg_ref.shape[1]
    size = messages[0].shape[1]
    pairs = [(keep_hbm, keep_ref), (exponent_hbm, exponent_ref), (seg_hbm, seg_ref)]
    for i, (first, many) in enumerate(chunks):
        wide = pl.ds(first * size, many * size)
        pairs += [(k_hbm.at[:, wide], k_refs[i]), (v_hbm.at[:, wide], v_refs[i])]
    copies = [pltpu.make_async_copy(*pair, sems.at[i]) for i, pair in enumerate(pairs)]
    for copy in copies:
        copy.start()
    earlier = lax.broadcasted_iota(jnp.int32, (tokens, tokens), 0)
    later = lax.broadcasted_iota(jnp.int32, (tokens, tokens), 1)
    upper = jnp.where(earlier <= later, 1.0, 0.0).astype(BF16)
    across = lax.broadcasted_iota(jnp.int32, (heads, heads), 1)
    down = lax.broadcasted_iota(jnp.int32, (heads, heads), 0)
    for copy in copies[:3]:
        copy.wait()
    spread = jnp.broadcast_to(exponent_ref[...], (heads, heads))
    exponent = jnp.sum(jnp.where(across == down, spread, 0).astype(F32), axis=1, keepdims=True)
    a = -jnp.exp2(-exponent) + jnp.log(keep_ref[...])
    high = a.astype(BF16)
    rest = a - high.astype(F32)
    middle = rest.astype(BF16)
    low = (rest - middle.astype(F32)).astype(BF16)
    parts = jnp.concatenate([high, middle, low], axis=0)
    sums = lax.dot_general(parts, upper, NN, preferred_element_type=F32)
    cumulative = sums[:heads] + (sums[heads : 2 * heads] + sums[2 * heads :])
    a_ref[...] = cumulative
    final = cumulative[:, tokens - 1 :]
    seg = seg_ref[...]
    last = seg[:, tokens - 1 :]
    w_ref[...] = jnp.where(seg == last, jnp.exp(final - cumulative), 0.0)
    for i, (first, many) in enumerate(chunks):
        copies[3 + 2 * i].wait()
        copies[4 + 2 * i].wait()
        finals = final[first : first + many]
        put_message(messages[i], first, many, size, w_ref, finals, last, k_refs[i], v_refs[i])


def message_of(size, many):
    return pltpu.VMEM((many * size + meta_rows(many), size), F32)


def first_messages(order, seg, exponent, keep, k, v, heads, chunks):
    tokens, size = k.shape[0], k.shape[1] // heads
    near = [pltpu.VMEM((tokens, many * size), BF16) for _, many in chunks]
    shapes = [message_of(size, many) for _, many in chunks]
    shapes += [pltpu.VMEM((heads, tokens), F32)] * 2 + [pltpu.VMEM((1, tokens), jnp.int32)]
    shapes += near + near
    number = len(chunks)
    out = pl.pallas_call(
        functools.partial(first_kernel, heads, chunks),
        in_specs=[pl.BlockSpec(memory_space=pltpu.SMEM)]
        + [pl.BlockSpec(memory_space=pltpu.HBM)] * 5,
        out_specs=[pl.BlockSpec(memory_space=pltpu.VMEM)] * len(shapes),
        out_shape=shapes,
        scratch_shapes=[
            pltpu.VMEM((1, heads), jnp.int32),
            pltpu.VMEM((heads, tokens), F32),
            pltpu.SemaphoreType.DMA((3 + 2 * number,)),
        ],
        compiler_params=pltpu.CompilerParams(vmem_limit_bytes=8 * MIB),
        cost_estimate=SHORT,
        name="first_messages",
    )(order, seg, exponent, keep, k, v)
    messages, (a, w, seg), out = out[:number], out[number : number + 3], out[number + 3 :]
    return messages, a, w, seg, out[:number], out[number:]


def rest_kernel(chunks, done, seg_ref, a_ref, w_ref, q_hbm, k_hbm, v_hbm, g_hbm, *refs):
    tokens = seg_ref.shape[1]
    left, number = chunks[done:], len(chunks)
    messages, mask_ref, refs, sems = refs[: len(left)], refs[len(left)], refs[len(left) + 1 : -1], refs[-1]
    k_refs, refs = refs[: len(left)], refs[len(left) :]
    v_refs, refs = refs[: len(left)], refs[len(left) :]
    q_refs, g_refs = refs[:number], refs[number:]
    size = messages[0].shape[1]
    pairs = []
    for i, (first, many) in enumerate(left):
        wide = pl.ds(first * size, many * size)
        pairs += [(k_hbm.at[:, wide], k_refs[i]), (v_hbm.at[:, wide], v_refs[i])]
    for i, (first, many) in enumerate(chunks):
        wide = pl.ds(first * size, many * size)
        pairs += [(q_hbm.at[:, wide], q_refs[i]), (g_hbm.at[:, wide], g_refs[i])]
    copies = [pltpu.make_async_copy(*pair, sems.at[i]) for i, pair in enumerate(pairs)]
    for copy in copies:
        copy.start()
    make_mask(seg_ref, mask_ref)
    last = seg_ref[:, tokens - 1 :]
    for i, (first, many) in enumerate(left):
        copies[2 * i].wait()
        copies[2 * i + 1].wait()
        final = a_ref[first : first + many, tokens - 1 :]
        put_message(messages[i], first, many, size, w_ref, final, last, k_refs[i], v_refs[i])
    for copy in copies[2 * len(left) :]:
        copy.wait()


def rest_messages(seg, a, w, q, k, v, g, chunks, done):
    heads = a.shape[0]
    tokens, size = k.shape[0], k.shape[1] // heads
    near = [pltpu.VMEM((tokens, many * size), BF16) for _, many in chunks]
    shapes = [message_of(size, many) for _, many in chunks[done:]]
    shapes += [pltpu.VMEM((tokens, tokens), F32)] + near[done:] * 2 + near * 2
    left, number = len(chunks) - done, len(chunks)
    out = pl.pallas_call(
        functools.partial(rest_kernel, chunks, done),
        in_specs=[pl.BlockSpec(memory_space=pltpu.VMEM)] * 3
        + [pl.BlockSpec(memory_space=pltpu.HBM)] * 4,
        out_specs=[pl.BlockSpec(memory_space=pltpu.VMEM)] * len(shapes),
        out_shape=shapes,
        scratch_shapes=[pltpu.SemaphoreType.DMA((2 * (left + number),))],
        compiler_params=pltpu.CompilerParams(vmem_limit_bytes=8 * MIB),
        cost_estimate=SHORT,
        name="rest_messages",
    )(seg, a, w, q, k, v, g)
    messages, mask, out = out[:left], out[left], out[left + 1 :]
    k_near, v_near, out = out[:left], out[left : 2 * left], out[2 * left :]
    return messages, mask, k_near, v_near, out[:number], out[number:]


def join_kernel(heads, order_ref, mine_ref, other_ref, out_ref):
    size = mine_ref.shape[1]
    top = heads * size
    mine_later = (order_ref[0] & 1) == 1
    final_mine, final_other = mine_ref[top : top + heads, :], other_ref[top : top + heads, :]
    end_mine, end_other = mine_ref[top + heads :, :], other_ref[top + heads :, :]
    same = jnp.where(end_mine[:1] == end_other[:1], 1.0, 0.0)
    scale_mine = jnp.where(mine_later, 1.0, jnp.exp(final_other) * same)
    scale_other = jnp.where(mine_later, jnp.exp(final_mine) * same, 1.0)
    for head in range(heads):
        rows = slice(head * size, (head + 1) * size)
        out_ref[rows, :] = (
            scale_mine[head : head + 1] * mine_ref[rows, :]
            + scale_other[head : head + 1] * other_ref[rows, :]
        )
    out_ref[top : top + heads, :] = final_mine + final_other
    out_ref[top + heads :, :] = jnp.where(mine_later, end_mine, end_other)


def small_call(kernel, name, order, first, second, after):
    vmem = pl.BlockSpec(memory_space=pltpu.VMEM)
    return pl.pallas_call(
        lambda order_ref, first_ref, second_ref, *rest: kernel(
            order_ref, first_ref, second_ref, rest[-1]
        ),
        in_specs=[pl.BlockSpec(memory_space=pltpu.SMEM), vmem, vmem]
        + [pl.BlockSpec(memory_space=pl.ANY)] * len(after),
        out_specs=vmem,
        out_shape=pltpu.VMEM(first.shape, F32),
        compiler_params=pltpu.CompilerParams(vmem_limit_bytes=8 * MIB),
        cost_estimate=SHORT,
        name=name,
    )(order, first, second, *after)


def joined(order, mine, other, heads, after=()):
    return small_call(
        functools.partial(join_kernel, heads), "join_windows", order, mine, other, after
    )


def pick_kernel(order_ref, even_ref, odd_ref, out_ref):
    odd = (order_ref[0] & 1) == 1

    @pl.when(odd)
    def _():
        out_ref[...] = odd_ref[...]

    @pl.when(jnp.logical_not(odd))
    def _():
        out_ref[...] = even_ref[...]


def picked(order, even, odd, after=()):
    return small_call(pick_kernel, "pick_message", order, even, odd, after)


def make_mask(seg_ref, mask_ref):
    tokens = seg_ref.shape[1]
    seg = seg_ref[...].astype(F32)
    column = as_column(seg, 128)
    for start in range(0, tokens, 128):
        across = lax.broadcasted_iota(jnp.int32, (tokens, 128), 1) + start
        down = lax.broadcasted_iota(jnp.int32, (tokens, 128), 0)
        seen = (column == seg[:, start : start + 128]) & (across <= down)
        mask_ref[:, start : start + 128] = jnp.where(seen, 0.0, -1e30)


def intra_kernel(
    first, heads, through, after, mask_ref, a_ref, gain_ref, q_ref, k_ref, v_ref, g_ref, *refs
):
    o_ref, gate_ref, *copied = refs[through + after :]
    for source, target in zip(refs[:through], copied):
        target[...] = source[...]
    tokens = mask_ref.shape[0]
    size = q_ref.shape[1] // heads
    block = min(tokens, 256)
    for j in range(heads):
        columns = slice(j * size, (j + 1) * size)
        a_row = a_ref[first + j : first + j + 1, :] * 1.4426950408889634
        a_column = as_column(a_row, 128)
        for start in range(0, tokens, block):
            here, upto = slice(start, start + block), slice(0, start + block)
            scores = lax.dot_general(
                q_ref[here, columns], k_ref[upto, columns], NT, preferred_element_type=F32
            )
            spread = jnp.concatenate([a_column[here]] * ((start + block) // 128), axis=1)
            weight = jnp.exp2(spread - a_row[:, upto] + mask_ref[here, upto])
            probs = (scores * weight).astype(BF16)
            o_ref[here, columns] = lax.dot_general(
                probs, v_ref[upto, columns], NN, preferred_element_type=F32
            )
        half = 0.5 * gain_ref[:, (first + j) * size : (first + j + 1) * size]
        gate_ref[:, columns] = half + half * jnp.tanh(0.5 * g_ref[:, columns].astype(F32))


def intra(mask, a, gain, q, k, v, g, first, heads, through=(), after=()):
    tokens, size = mask.shape[0], gain.shape[1] // a.shape[0]
    vmem = pl.BlockSpec(memory_space=pltpu.VMEM)
    o, gate, *copied = pl.pallas_call(
        functools.partial(intra_kernel, first, heads, len(through), len(after)),
        in_specs=[vmem] * (7 + len(through)) + [pl.BlockSpec(memory_space=pl.ANY)] * len(after),
        out_specs=[vmem] * (2 + len(through)),
        out_shape=[pltpu.VMEM((tokens, heads * size), F32)] * 2
        + [pltpu.VMEM(x.shape, x.dtype) for x in through],
        compiler_params=pltpu.CompilerParams(vmem_limit_bytes=8 * MIB),
        cost_estimate=SHORT,
        name="intra_span",
    )(mask, a, gain, q, k, v, g, *through, *after)
    return (o, gate, q), copied


def final_kernel(
    first,
    heads,
    kind,
    unread,
    order_ref,
    seg_ref,
    own_ref,
    near_ref,
    past_ref,
    o_ref,
    gate_ref,
    q_ref,
    a_ref,
    *rest,
):
    gated_hbm, snap_hbm, gated_ref, snap_ref, sems = rest[unread:]
    tokens, size = q_ref.shape[0], own_ref.shape[1]
    block = min(tokens, 256)
    top = heads * size
    place = order_ref[0]
    ends = slice(top + heads, top + heads + 1)
    finals = slice(top, top + heads)
    own_end, near_end, past_end = own_ref[ends, :], near_ref[ends, :], past_ref[ends, :]
    bridged = jnp.exp(near_ref[finals, :]) * jnp.where(near_end == past_end, 1.0, 0.0)
    if kind == "pair":
        odd = (place & 1) == 1
        previous = jnp.where(odd, near_end, past_end)
        scale_near = jnp.where(odd, 1.0, 0.0)
        scale_past = jnp.where(odd, bridged, 1.0)
    else:
        previous = near_end
        scale_near = jnp.where(place > 0, 1.0, 0.0)
        scale_past = bridged
    scale_past = jnp.where(place >= 2, scale_past, 0.0)
    own_decay = jnp.exp(own_ref[finals, :]) * jnp.where(own_end == previous, 1.0, 0.0)
    valid = seg_ref[...].astype(F32) == previous[:, :1]
    copies = []
    for j in range(heads):
        rows = columns = slice(j * size, (j + 1) * size)
        state = scale_past[j : j + 1] * past_ref[rows, :] + scale_near * near_ref[rows, :]
        snap_ref[j] = own_decay[j : j + 1] * state + own_ref[rows, :]
        high = state.astype(BF16)
        low = (state - high.astype(F32)).astype(BF16)
        q = q_ref[:, columns]
        both = jnp.concatenate([high, low], axis=0)
        decay = jnp.where(valid, jnp.exp(a_ref[first + j : first + j + 1, :]), 0.0)
        decay = as_column(decay, size)
        for start in range(0, tokens, block):
            here = slice(start, start + block)
            inter = lax.dot_general(
                jnp.concatenate([q[here], q[here]], axis=1), both, NN, preferred_element_type=F32
            )
            mixed = o_ref[here, columns] + inter * decay[here]
            mean_square = jnp.mean(mixed * mixed, axis=1, keepdims=True)
            gated = mixed * lax.rsqrt(mean_square + 1e-06) * gate_ref[here, columns]
            gated_ref[here, columns] = gated.astype(BF16)
        if j % 2 == 1 or j == heads - 1:
            begin = j - j % 2
            width = (j + 1 - begin) * size
            heads_here = pl.ds(first + begin, j + 1 - begin)
            place = pl.ds((first + begin) * size, width)
            for source, target in (
                (gated_ref.at[:, pl.ds(begin * size, width)], gated_hbm.at[:, place]),
                (snap_ref.at[pl.ds(begin, j + 1 - begin)], snap_hbm.at[0, heads_here]),
            ):
                copies.append(pltpu.make_async_copy(source, target, sems.at[len(copies)]))
                copies[-1].start()
    for copy in copies:
        copy.wait()


def finish(order, seg, own, near, past, o, gate, q, a, so_far, after, first, heads, kind):
    tokens, size = q.shape[0], q.shape[1] // heads
    total = a.shape[0]
    vmem, anywhere = pl.BlockSpec(memory_space=pltpu.VMEM), pl.BlockSpec(memory_space=pl.ANY)
    unread = len(so_far) + len(after)
    return pl.pallas_call(
        functools.partial(final_kernel, first, heads, kind, unread),
        in_specs=[pl.BlockSpec(memory_space=pltpu.SMEM)] + [vmem] * 8 + [anywhere] * unread,
        out_specs=[anywhere, anywhere],
        out_shape=[
            jax.ShapeDtypeStruct((tokens, total * size), BF16),
            jax.ShapeDtypeStruct((1, total, size, size), F32),
        ],
        scratch_shapes=[
            pltpu.VMEM((tokens, heads * size), BF16),
            pltpu.VMEM((heads, size, size), F32),
            pltpu.SemaphoreType.DMA((2 * heads,)),
        ],
        input_output_aliases={9 + i: i for i in range(len(so_far))},
        compiler_params=pltpu.CompilerParams(vmem_limit_bytes=8 * MIB),
        cost_estimate=SHORT,
        name="finish",
    )(order, seg, own, near, past, o, gate, q, a, *so_far, *after)


def shards(q, k, v, g, segment, decay_exponent, retention, norm_gain):
    heads = decay_exponent.shape[0]
    tokens = q.shape[0]
    count = lax.axis_size("seq")
    place = lax.axis_index("seq")
    reach = max(1, count // 4)
    far = lambda x: pltpu.with_memory_space_constraint(x, pltpu.HBM)
    q, k, v, g = far(q), far(k), far(v), far(g)
    gain = norm_gain.reshape(1, -1)
    order = jnp.where(place >= 2, 2 + (place & 1), place & 1).astype(jnp.int32).reshape(1)
    later = jnp.ones((1,), jnp.int32)
    swap = lambda x: lax.ppermute(x, "seq", [(c, c ^ 1) for c in range(count)])
    turn = lambda x: lax.ppermute(x, "seq", [(c, (c + 2) % count) for c in range(count)])

    half = heads // 2
    small = half * 3 // 8
    big = half - small
    chunks = [(0, big), (half, big), (big, small), (half + big, small)]

    def widened(x, many, shift, window):
        while window < reach:
            past = lax.ppermute(x, "seq", [(c, c + shift) for c in range(count - shift)])
            x = joined(later, x, past, many)
            shift, window = 2 * shift, 2 * window
        return x

    own, a, w, seg, k_near, v_near = first_messages(
        order,
        far(segment.reshape(1, tokens)),
        far(decay_exponent.reshape(1, heads)),
        far(retention),
        k,
        v,
        heads,
        chunks[:2],
    )
    near, past, inside = {}, {}, {}
    near[1] = swap(own[1])
    past[0] = turn(own[0])
    messages, mask, k_rest, v_rest, q_near, g_near = rest_messages(
        seg, a, w, q, k, v, g, chunks, 2
    )
    own, k_near, v_near = [*own, *messages], [*k_near, *k_rest], [*v_near, *v_rest]

    def look_inside(i, through=(), after=()):
        inside[i], copied = intra(
            mask, a, gain, q_near[i], k_near[i], v_near[i], g_near[i], *chunks[i], through, after
        )
        return copied

    own[2], own[3] = look_inside(0, (own[2], own[3]))
    past[2] = turn(own[2])
    near[3] = swap(own[3])
    look_inside(1, (), (own[2], own[3]))

    def second_hops(i, after):
        picks = picked(order, own[i], past[i], after)
        near[i] = swap(picks)
        both = joined(order, own[i + 1], near[i + 1], chunks[i + 1][1], (picks,))
        past[i + 1] = turn(both)
        return both

    both = second_hops(0, (inside[1][0],))
    look_inside(2, (), (both,))
    look_inside(3, (), (both,))
    both = second_hops(2, (inside[2][0], inside[3][0]))

    if reach > 2:
        for i, (_, many) in enumerate(chunks):
            if i % 2 == 0:
                near[i] = jnp.where(place >= 1, near[i], 0.0)
                past[i] = jnp.where(place >= 2, past[i], 0.0)
                near[i] = widened(joined(later, near[i], past[i], many), many, 2, 2)
                past[i] = jnp.zeros_like(near[i])
            else:
                past[i] = widened(jnp.where(place >= 2, past[i], 0.0), many, 2, 2)

    result = ()
    for i, (first, many) in enumerate(chunks):
        result = finish(
            order, seg, own[i], near[i], past[i], *inside[i], a, result, (both,), first, many,
            ("span", "pair")[i % 2],
        )
    return tuple(result)


def solution(mesh):
    placed = (
        P(("groups", "seq"), "wt"),
        P(("groups", "seq"), "wt"),
        P(("groups", "seq"), "wt"),
        P(("groups", "seq"), "wt"),
        P(("groups", "seq")),
        P("wt"),
        P("wt", ("groups", "seq")),
        P("wt"),
    )
    return jax.shard_map(
        shards,
        mesh=mesh,
        in_specs=placed,
        out_specs=(P(("groups", "seq"), "wt"), P(("groups", "seq"), "wt", None, None)),
        check_vma=False,
    )
```

time: 43.1 us -> 35.3 us (0.82)
  waiting for transfers between devices: 10.3 us -> 4.48 us
  starting transfers between devices: 14 us -> 12.1 us
    ppermute x8, waiting for transfers between devices: 10.3 us -> 4.48 us  [the longest x4 4.47 us: shards(): swap = lambda x: lax.ppermute(x, 'seq', [(c, c ^ 1) for c in range(count)])]
    ppermute x8, starting transfers between devices: 14 us -> 12.1 us  [the longest x4 7.38 us: shards(): lax.ppermute(x, 'seq', [(c, (c + 2) % count) for c in range(count)])]
  transfers between devices with their start and end apart: 8 -> 8, of which waited for: 6 -> 1; matrix products, arithmetic and copies ran while one was open for 0% -> 0% of each run, Pallas kernels for 34% -> 40%
where the time goes in v1:
time: 35.3 us; the launch traced here: 35.2 us
  Pallas kernels  17.8 us (50%)
  starting transfers between devices  12.1 us (34%)
  waiting for transfers between devices  4.48 us (13%)
  between operations  0.77 us (2%)
    ppermute x4, starting transfers between devices, shards(): lax.ppermute(x, 'seq', [(c, (c + 2) % count) for c in range(count)])  7.38 us
    pallas_call x4, Pallas kernels, finish(): pl.pallas_call(functools.partial(final_kernel, first, heads, kind, unread...  6.57 us
    pallas_call x4, Pallas kernels, intra(): pl.pallas_call(functools.partial(intra_kernel, first, heads, len(through)...  6.06 us
    ppermute x4, starting transfers between devices, shards(): swap = lambda x: lax.ppermute(x, 'seq', [(c, c ^ 1) for c in range(count)])  4.75 us
    ppermute x4, waiting for transfers between devices, shards(): swap = lambda x: lax.ppermute(x, 'seq', [(c, c ^ 1) for c in range(count)])  4.47 us
    pallas_call x1, Pallas kernels, rest_messages(): pl.pallas_call(functools.partial(rest_kernel, chunks, done), in_specs=[pl...  2.81 us
    pallas_call x1, Pallas kernels, first_messages(): pl.pallas_call(functools.partial(first_kernel, heads, chunks), in_specs=[...  2.2 us
  transfers between devices with their start and end apart: 8, of which 1 were waited for; matrix products, arithmetic and copies ran while one was open for 0% of the time, Pallas kernels for 40%

profile of v1, /device:TPU:0, one launch (start us, length us, event | category | flops | bytes accessed | tf_op | source)
XLA Modules:
  0.0 35.2 jit_solution(18277841080002200937)
XLA Ops:
  0.6 2.2 %first_messages.1 = (f32[648,128]{1,0:T(8,128)S(1)}, f32[648,128]{1,0:T(8,128)S(1)}, f32[16,512]{1,0:T(8,128)S(1)}, f32[16,512]{1,0:T(8,128)S(1)}, s32[1,512]{1,...) custom-call(s32[1]{0:T(128)} %bitcast.order_ref, ...), custom_call_target="tpu_custom_call" | custom-call | flops 1 | bytes 1 | tf_op jit(solution)/shard_map/first_messages/pallas_call | solution.py:99
  2.9 3.1 %collective-permute-start.3 = (f32[648,128]{1,0:T(8,128)S(1)}, f32[648,128]{1,0:T(8,128)S(1)}, u32[]{:S(2)}, u32[]{:S(2)}) collective-permute-start(f32[648,128]{1,0:T(8,128)S(1)} %get-tuple-element.59.first_ref.own_ref), channel_id=1, source_target_pairs={{0,4},{2,6},{4,8},{6,10},{8,12},{10,14},{12,0},{14,2},{1,5},{3,7},... | collective-permute-start | bytes 995336 | tf_op jit(solution)/shard_map/ppermute | solution.py:391
  5.9 1.5 %collective-permute-start.2 = (f32[648,128]{1,0:T(8,128)S(1)}, f32[648,128]{1,0:T(8,128)S(1)}, u32[]{:S(2)}, u32[]{:S(2)}) collective-permute-start(f32[648,128]{1,0:T(8,128)S(1)} %get-tuple-element.58.first_ref.own_ref), channel_id=1, source_target_pairs={{0,2},{2,0},{4,6},{6,4},{8,10},{10,8},{12,14},{14,12},{1,3},{3,1},... | collective-permute-start | bytes 995336 | tf_op jit(solution)/shard_map/ppermute | solution.py:390
  7.4 2.8 %rest_messages.1 = (f32[392,128]{1,0:T(8,128)S(1)}, f32[392,128]{1,0:T(8,128)S(1)}, f32[512,512]{1,0:T(8,128)S(1)}, bf16[512,384]{1,0:T(8,128)(2,1)S(1)}, bf16[5...) custom-call(s32[1,512]{1,0:T(1,128)S(1)} %get-tuple-element.42.seg_r, ...), custom_call_target="tpu_custom_call" | custom-call | flops 1 | bytes 1 | tf_op jit(solution)/shard_map/rest_messages/pallas_call | solution.py:154
  10.3 1.8 %intra_span.4 = (f32[512,640]{1,0:T(8,128)S(1)}, f32[512,640]{1,0:T(8,128)S(1)}, f32[392,128]{1,0:T(8,128)S(1)}, f32[392,128]{1,0:T(8,128)S(1)}) custom-call(f32[512,512]{1,0:T(8,128)S(1)} %get-tuple-element.45.mask_ref, f32[16,512]{1,0:T(8,128)S(1)} %get-tuple-element.43.a_ref, f32[1,2048]{1,0:T(1,128)S(1)} %bitcast.4, ...), custom_call_target="tpu_custom_call" | custom-call | flops 1 | bytes 1 | tf_op jit(solution)/shard_map/intra_span/pallas_call | solution.py:269
  12.1 1.6 %collective-permute-start.1 = (f32[392,128]{1,0:T(8,128)S(1)}, f32[392,128]{1,0:T(8,128)S(1)}, u32[]{:S(2)}, u32[]{:S(2)}) collective-permute-start(f32[392,128]{1,0:T(8,128)S(1)} %get-tuple-element.53.refs_0_.first_ref.own_ref), channel_id=1, source_target_pairs={{0,4},{2,6},{4,8},{6,10},{8,12},{10,14},{12,0},{14,2},{1,5},{3,7},... | collective-permute-start | bytes 602120 | tf_op jit(solution)/shard_map/ppermute | solution.py:391
  13.7 0.5 %collective-permute-start = (f32[392,128]{1,0:T(8,128)S(1)}, f32[392,128]{1,0:T(8,128)S(1)}, u32[]{:S(2)}, u32[]{:S(2)}) collective-permute-start(f32[392,128]{1,0:T(8,128)S(1)} %get-tuple-element.52.refs_1_.first_ref.own_ref), channel_id=1, source_target_pairs={{0,2},{2,0},{4,6},{6,4},{8,10},{10,8},{12,14},{14,12},{1,3},{3,1},... | collective-permute-start | bytes 602120 | tf_op jit(solution)/shard_map/ppermute | solution.py:390
  14.2 1.8 %intra_span.5 = (f32[512,640]{1,0:T(8,128)S(1)}, f32[512,640]{1,0:T(8,128)S(1)}) custom-call(f32[512,512]{1,0:T(8,128)S(1)} %get-tuple-element.45.mask_ref, f32[16,512]{1,0:T(8,128)S(1)} %get-tuple-element.43.a_ref, f32[1,2048]{1,0:T(1,128)S(1)} %bitcast.5, bf16[512,640]{1,0:T(8,128)(2,1)S(1)} %get-tuple-element.60.q_ref, ...), custom_call_target="tpu_custom_call" | custom-call | flops 1 | bytes 1 | tf_op jit(solution)/shard_map/intra_span/pallas_call | solution.py:269
  16.1 2.1 %collective-permute-start.7 = (f32[648,128]{1,0:T(8,128)S(1)}, f32[648,128]{1,0:T(8,128)S(1)}, u32[]{:S(2)}, u32[]{:S(2)}) collective-permute-start(f32[648,128]{1,0:T(8,128)S(1)} %pick_message.2.rest_0_), channel_id=1, source_target_pairs={{0,2},{2,0},{4,6},{6,4},{8,10},{10,8},{12,14},{14,12},{1,3},{3,1},... | collective-permute-start | bytes 995336 | tf_op jit(solution)/shard_map/ppermute | solution.py:390
  18.2 0.0 collective-permute-done.2.second_ref.near_ref
  18.2 0.1 join_windows.2.refs_0_
  18.3 1.1 %collective-permute-start.6 = (f32[648,128]{1,0:T(8,128)S(1)}, f32[648,128]{1,0:T(8,128)S(1)}, u32[]{:S(2)}, u32[]{:S(2)}) collective-permute-start(f32[648,128]{1,0:T(8,128)S(1)} %join_windows.2.refs_0_), channel_id=1, source_target_pairs={{0,4},{2,6},{4,8},{6,10},{8,12},{10,14},{12,0},{14,2},{1,5},{3,7},... | collective-permute-start | bytes 995336 | tf_op jit(solution)/shard_map/ppermute | solution.py:391
  19.3 1.2 %intra_span.7 = (f32[512,384]{1,0:T(8,128)S(1)}, f32[512,384]{1,0:T(8,128)S(1)}) custom-call(f32[512,512]{1,0:T(8,128)S(1)} %get-tuple-element.45.mask_ref, f32[16,512]{1,0:T(8,128)S(1)} %get-tuple-element.43.a_ref, f32[1,2048]{1,0:T(1,128)S(1)} %bitcast.6, bf16[512,384]{1,0:T(8,128)(2,1)S(1)} %get-tuple-element.66.q_ref, ...), custom_call_target="tpu_custom_call" | custom-call | flops 1 | bytes 1 | tf_op jit(solution)/shard_map/intra_span/pallas_call | solution.py:269
  20.6 1.2 %intra_span.6 = (f32[512,384]{1,0:T(8,128)S(1)}, f32[512,384]{1,0:T(8,128)S(1)}) custom-call(f32[512,512]{1,0:T(8,128)S(1)} %get-tuple-element.45.mask_ref, f32[16,512]{1,0:T(8,128)S(1)} %get-tuple-element.43.a_ref, f32[1,2048]{1,0:T(1,128)S(1)} %bitcast.7, bf16[512,384]{1,0:T(8,128)(2,1)S(1)} %get-tuple-element.54.q_ref, ...), custom_call_target="tpu_custom_call" | custom-call | flops 1 | bytes 1 | tf_op jit(solution)/shard_map/intra_span/pallas_call | solution.py:269
  21.9 0.6 %collective-permute-start.5 = (f32[392,128]{1,0:T(8,128)S(1)}, f32[392,128]{1,0:T(8,128)S(1)}, u32[]{:S(2)}, u32[]{:S(2)}) collective-permute-start(f32[392,128]{1,0:T(8,128)S(1)} %pick_message.3.rest_0_), channel_id=1, source_target_pairs={{0,2},{2,0},{4,6},{6,4},{8,10},{10,8},{12,14},{14,12},{1,3},{3,1},... | collective-permute-start | bytes 602120 | tf_op jit(solution)/shard_map/ppermute | solution.py:390
  22.4 0.0 collective-permute-done.second_ref.near_ref
  22.5 1.6 %collective-permute-start.4 = (f32[392,128]{1,0:T(8,128)S(1)}, f32[392,128]{1,0:T(8,128)S(1)}, u32[]{:S(2)}, u32[]{:S(2)}) collective-permute-start(f32[392,128]{1,0:T(8,128)S(1)} %join_windows.3.rest_0_.rest_2_), channel_id=1, source_target_pairs={{0,4},{2,6},{4,8},{6,10},{8,12},{10,14},{12,0},{14,2},{1,5},{3,7},... | collective-permute-start | bytes 602120 | tf_op jit(solution)/shard_map/ppermute | solution.py:391
  24.1 4.5 %collective-permute-done.7.near_ref = f32[648,128]{1,0:T(8,128)S(1)} collective-permute-done((f32[648,128]{1,0:T(8,128)S(1)}, f32[648,128]{1,0:T(8,128)S(1)}, u32[]{:S(2)}, u32[]{:S(2)}) %collective-permute-start.7) | collective-permute-done | bytes 331808 | tf_op jit(solution)/shard_map/ppermute | solution.py:390
  28.6 1.8 %finish.4 = (bf16[512,2048]{1,0:T(8,128)(2,1)}, f32[1,16,128,128]{3,2,1,0:T(8,128)}) custom-call(s32[1]{0:T(128)} %bitcast.order_ref, s32[1,512]{1,0:T(1,128)S(1)} %get-tuple-element.42.seg_ref, f32[648,128]{1,0:T(8,128)S(1)} %get-tuple-element.59.first_ref.own_ref, f32[648,128]{1,0:T(8,128)S(1)} %collective-permute-done.7.near_ref, ...), custom_call_target="tpu_custom_call" | custom-call | flops 1 | bytes 1 | tf_op jit(solution)/shard_map/finish/pallas_call | solution.py:359
  30.4 0.0 collective-permute-done.6.past_ref
  30.4 1.8 %finish.5 = (bf16[512,2048]{1,0:T(8,128)(2,1)}, f32[1,16,128,128]{3,2,1,0:T(8,128)}) custom-call(s32[1]{0:T(128)} %bitcast.order_ref, s32[1,512]{1,0:T(1,128)S(1)} %get-tuple-element.42.seg_ref, f32[648,128]{1,0:T(8,128)S(1)} %get-tuple-element.58.first_ref.own_ref, ...), custom_call_target="tpu_custom_call", output_to_operand_aliasing={{0}: (9, {}), {1}: (10, {})} | custom-call | flops 1 | bytes 1 | tf_op jit(solution)/shard_map/finish/pallas_call | solution.py:359
  32.3 1.5 %finish.6 = (bf16[512,2048]{1,0:T(8,128)(2,1)}, f32[1,16,128,128]{3,2,1,0:T(8,128)}) custom-call(s32[1]{0:T(128)} %bitcast.order_ref, s32[1,512]{1,0:T(1,128)S(1)} %get-tuple-element.42.seg_ref, f32[392,128]{1,0:T(8,128)S(1)} %get-tuple-element.53.refs_0_.first_ref.own_ref, ...), custom_call_target="tpu_custom_call", output_to_operand_aliasing={{0}: (9, {}), {1}: (10, {})} | custom-call | flops 1 | bytes 1 | tf_op jit(solution)/shard_map/finish/pallas_call | solution.py:359
  33.7 0.0 collective-permute-done.4.past_ref
  33.7 1.4 %finish.7 = (bf16[512,2048]{1,0:T(8,128)(2,1)}, f32[1,16,128,128]{3,2,1,0:T(8,128)}) custom-call(s32[1]{0:T(128)} %bitcast.order_ref, s32[1,512]{1,0:T(1,128)S(1)} %get-tuple-element.42.seg_ref, f32[392,128]{1,0:T(8,128)S(1)} %get-tuple-element.52.refs_1_.first_ref.own_ref, ...), custom_call_target="tpu_custom_call", output_to_operand_aliasing={{0}: (9, {}), {1}: (10, {})} | custom-call | flops 1 | bytes 1 | tf_op jit(solution)/shard_map/finish/pallas_call | solution.py:359
  (8 shorter events, 0.1 us)
Async XLA Ops:
  2.9 13.2 %collective-permute-start.3 = (f32[648,128]{1,0:T(8,128)S(1)}, f32[648,128]{1,0:T(8,128)S(1)}, u32[]{:S(2)}, u32[]{:S(2)}) collective-permute-start(f32[648,128]{1,0:T(8,128)S(1)} %get-tuple-element.59.first_ref.own_ref), channel_id=1, source_target_pairs={{0,4},{2,6},{4,8},{6,10},{8,12},{10,14},{12,0},{14,2},{1,5},{3,7},... | collective-permute-start | bytes 995336 | tf_op jit(solution)/shard_map/ppermute | solution.py:391
  5.9 12.3 %collective-permute-start.2 = (f32[648,128]{1,0:T(8,128)S(1)}, f32[648,128]{1,0:T(8,128)S(1)}, u32[]{:S(2)}, u32[]{:S(2)}) collective-permute-start(f32[648,128]{1,0:T(8,128)S(1)} %get-tuple-element.58.first_ref.own_ref), channel_id=1, source_target_pairs={{0,2},{2,0},{4,6},{6,4},{8,10},{10,8},{12,14},{14,12},{1,3},{3,1},... | collective-permute-start | bytes 995336 | tf_op jit(solution)/shard_map/ppermute | solution.py:390
  7.4 2.8 %copy-start = (f32[2048]{0:T(1024)S(1)}, f32[2048]{0:T(1024)}, u32[]{:S(2)}) copy-start(f32[2048]{0:T(1024)} %param.15) | copy-start | bytes 24580
  12.1 9.8 %collective-permute-start.1 = (f32[392,128]{1,0:T(8,128)S(1)}, f32[392,128]{1,0:T(8,128)S(1)}, u32[]{:S(2)}, u32[]{:S(2)}) collective-permute-start(f32[392,128]{1,0:T(8,128)S(1)} %get-tuple-element.53.refs_0_.first_ref.own_ref), channel_id=1, source_target_pairs={{0,4},{2,6},{4,8},{6,10},{8,12},{10,14},{12,0},{14,2},{1,5},{3,7},... | collective-permute-start | bytes 602120 | tf_op jit(solution)/shard_map/ppermute | solution.py:391
  13.7 8.8 %collective-permute-start = (f32[392,128]{1,0:T(8,128)S(1)}, f32[392,128]{1,0:T(8,128)S(1)}, u32[]{:S(2)}, u32[]{:S(2)}) collective-permute-start(f32[392,128]{1,0:T(8,128)S(1)} %get-tuple-element.52.refs_1_.first_ref.own_ref), channel_id=1, source_target_pairs={{0,2},{2,0},{4,6},{6,4},{8,10},{10,8},{12,14},{14,12},{1,3},{3,1},... | collective-permute-start | bytes 602120 | tf_op jit(solution)/shard_map/ppermute | solution.py:390
  16.1 12.5 %collective-permute-start.7 = (f32[648,128]{1,0:T(8,128)S(1)}, f32[648,128]{1,0:T(8,128)S(1)}, u32[]{:S(2)}, u32[]{:S(2)}) collective-permute-start(f32[648,128]{1,0:T(8,128)S(1)} %pick_message.2.rest_0_), channel_id=1, source_target_pairs={{0,2},{2,0},{4,6},{6,4},{8,10},{10,8},{12,14},{14,12},{1,3},{3,1},... | collective-permute-start | bytes 995336 | tf_op jit(solution)/shard_map/ppermute | solution.py:390
  18.3 12.1 %collective-permute-start.6 = (f32[648,128]{1,0:T(8,128)S(1)}, f32[648,128]{1,0:T(8,128)S(1)}, u32[]{:S(2)}, u32[]{:S(2)}) collective-permute-start(f32[648,128]{1,0:T(8,128)S(1)} %join_windows.2.refs_0_), channel_id=1, source_target_pairs={{0,4},{2,6},{4,8},{6,10},{8,12},{10,14},{12,0},{14,2},{1,5},{3,7},... | collective-permute-start | bytes 995336 | tf_op jit(solution)/shard_map/ppermute | solution.py:391
  21.9 10.4 %collective-permute-start.5 = (f32[392,128]{1,0:T(8,128)S(1)}, f32[392,128]{1,0:T(8,128)S(1)}, u32[]{:S(2)}, u32[]{:S(2)}) collective-permute-start(f32[392,128]{1,0:T(8,128)S(1)} %pick_message.3.rest_0_), channel_id=1, source_target_pairs={{0,2},{2,0},{4,6},{6,4},{8,10},{10,8},{12,14},{14,12},{1,3},{3,1},... | collective-permute-start | bytes 602120 | tf_op jit(solution)/shard_map/ppermute | solution.py:390
  22.5 11.2 %collective-permute-start.4 = (f32[392,128]{1,0:T(8,128)S(1)}, f32[392,128]{1,0:T(8,128)S(1)}, u32[]{:S(2)}, u32[]{:S(2)}) collective-permute-start(f32[392,128]{1,0:T(8,128)S(1)} %join_windows.3.rest_0_.rest_2_), channel_id=1, source_target_pairs={{0,4},{2,6},{4,8},{6,10},{8,12},{10,14},{12,0},{14,2},{1,5},{3,7},... | collective-permute-start | bytes 602120 | tf_op jit(solution)/shard_map/ppermute | solution.py:391

commit v2 on v1

--- a/solution.py
+++ b/solution.py
@@ -279,101 +279,97 @@
     return (o, gate, q), copied
 
 
-def final_kernel(
-    first,
-    heads,
-    kind,
-    unread,
-    order_ref,
-    seg_ref,
-    own_ref,
-    near_ref,
-    past_ref,
-    o_ref,
-    gate_ref,
-    q_ref,
-    a_ref,
-    *rest,
-):
-    gated_hbm, snap_hbm, gated_ref, snap_ref, sems = rest[unread:]
-    tokens, size = q_ref.shape[0], own_ref.shape[1]
-    block = min(tokens, 256)
-    top = heads * size
+def final_kernel(groups, unread, order_ref, seg_ref, a_ref, *rest):
+    number = len(groups)
+    inputs, rest = rest[: 6 * number], rest[6 * number + unread :]
+    gated_hbm, snap_hbm, *scratch, sems = rest
     place = order_ref[0]
-    ends = slice(top + heads, top + heads + 1)
-    finals = slice(top, top + heads)
-    own_end, near_end, past_end = own_ref[ends, :], near_ref[ends, :], past_ref[ends, :]
-    bridged = jnp.exp(near_ref[finals, :]) * jnp.where(near_end == past_end, 1.0, 0.0)
-    if kind == "pair":
-        odd = (place & 1) == 1
-        previous = jnp.where(odd, near_end, past_end)
-        scale_near = jnp.where(odd, 1.0, 0.0)
-        scale_past = jnp.where(odd, bridged, 1.0)
-    else:
-        previous = near_end
-        scale_near = jnp.where(place > 0, 1.0, 0.0)
-        scale_past = bridged
-    scale_past = jnp.where(place >= 2, scale_past, 0.0)
-    own_decay = jnp.exp(own_ref[finals, :]) * jnp.where(own_end == previous, 1.0, 0.0)
-    valid = seg_ref[...].astype(F32) == previous[:, :1]
+    seg = seg_ref[...].astype(F32)
     copies = []
-    for j in range(heads):
-        rows = columns = slice(j * size, (j + 1) * size)
-        state = scale_past[j : j + 1] * past_ref[rows, :] + scale_near * near_ref[rows, :]
-        snap_ref[j] = own_decay[j : j + 1] * state + own_ref[rows, :]
-        high = state.astype(BF16)
-        low = (state - high.astype(F32)).astype(BF16)
-        q = q_ref[:, columns]
-        both = jnp.concatenate([high, low], axis=0)
-        decay = jnp.where(valid, jnp.exp(a_ref[first + j : first + j + 1, :]), 0.0)
-        decay = as_column(decay, size)
-        for start in range(0, tokens, block):
-            here = slice(start, start + block)
-            inter = lax.dot_general(
-                jnp.concatenate([q[here], q[here]], axis=1), both, NN, preferred_element_type=F32
-            )
-            mixed = o_ref[here, columns] + inter * decay[here]
-            mean_square = jnp.mean(mixed * mixed, axis=1, keepdims=True)
-            gated = mixed * lax.rsqrt(mean_square + 1e-06) * gate_ref[here, columns]
-            gated_ref[here, columns] = gated.astype(BF16)
-        if j % 2 == 1 or j == heads - 1:
-            begin = j - j % 2
-            width = (j + 1 - begin) * size
-            heads_here = pl.ds(first + begin, j + 1 - begin)
-            place = pl.ds((first + begin) * size, width)
-            for source, target in (
-                (gated_ref.at[:, pl.ds(begin * size, width)], gated_hbm.at[:, place]),
-                (snap_ref.at[pl.ds(begin, j + 1 - begin)], snap_hbm.at[0, heads_here]),
-            ):
-                copies.append(pltpu.make_async_copy(source, target, sems.at[len(copies)]))
-                copies[-1].start()
+    for i, (first, heads, kind) in enumerate(groups):
+        own_ref, near_ref, past_ref, o_ref, gate_ref, q_ref = inputs[6 * i : 6 * i + 6]
+        gated_ref, snap_ref = scratch[2 * i : 2 * i + 2]
+        tokens, size = q_ref.shape[0], own_ref.shape[1]
+        block = min(tokens, 256)
+        top = heads * size
+        ends = slice(top + heads, top + heads + 1)
+        finals = slice(top, top + heads)
+        own_end, near_end, past_end = own_ref[ends, :], near_ref[ends, :], past_ref[ends, :]
+        bridged = jnp.exp(near_ref[finals, :]) * jnp.where(near_end == past_end, 1.0, 0.0)
+        if kind == "pair":
+            odd = (place & 1) == 1
+            previous = jnp.where(odd, near_end, past_end)
+            scale_near = jnp.where(odd, 1.0, 0.0)
+            scale_past = jnp.where(odd, bridged, 1.0)
+        else:
+            previous = near_end
+            scale_near = jnp.where(place > 0, 1.0, 0.0)
+            scale_past = bridged
+        scale_past = jnp.where(place >= 2, scale_past, 0.0)
+        own_decay = jnp.exp(own_ref[finals, :]) * jnp.where(own_end == previous, 1.0, 0.0)
+        valid = seg == previous[:, :1]
+        for j in range(heads):
+            rows = columns = slice(j * size, (j + 1) * size)
+            state = scale_past[j : j + 1] * past_ref[rows, :] + scale_near * near_ref[rows, :]
+            snap_ref[j] = own_decay[j : j + 1] * state + own_ref[rows, :]
+            high = state.astype(BF16)
+            low = (state - high.astype(F32)).astype(BF16)
+            q = q_ref[:, columns]
+            both = jnp.concatenate([high, low], axis=0)
+            decay = jnp.where(valid, jnp.exp(a_ref[first + j : first + j + 1, :]), 0.0)
+            decay = as_column(decay, size)
+            for start in range(0, tokens, block):
+                here = slice(start, start + block)
+                inter = lax.dot_general(
+                    jnp.concatenate([q[here], q[here]], axis=1),
+                    both,
+                    NN,
+                    preferred_element_type=F32,
+                )
+                mixed = o_ref[here, columns] + inter * decay[here]
+                mean_square = jnp.mean(mixed * mixed, axis=1, keepdims=True)
+                gated = mixed * lax.rsqrt(mean_square + 1e-06) * gate_ref[here, columns]
+                gated_ref[here, columns] = gated.astype(BF16)
+            if j % 2 == 1 or j == heads - 1:
+                begin = j - j % 2
+                width = (j + 1 - begin) * size
+                heads_here = pl.ds(first + begin, j + 1 - begin)
+                there = pl.ds((first + begin) * size, width)
+                for source, target in (
+                    (gated_ref.at[:, pl.ds(begin * size, width)], gated_hbm.at[:, there]),
+                    (snap_ref.at[pl.ds(begin, j + 1 - begin)], snap_hbm.at[0, heads_here]),
+                ):
+                    copies.append(pltpu.make_async_copy(source, target, sems.at[len(copies)]))
+                    copies[-1].start()
     for copy in copies:
         copy.wait()
 
 
-def finish(order, seg, own, near, past, o, gate, q, a, so_far, after, first, heads, kind):
-    tokens, size = q.shape[0], q.shape[1] // heads
-    total = a.shape[0]
+def finish(order, seg, a, groups, arrays, so_far, after):
+    total, tokens = a.shape
+    size = arrays[0].shape[1]
     vmem, anywhere = pl.BlockSpec(memory_space=pltpu.VMEM), pl.BlockSpec(memory_space=pl.ANY)
     unread = len(so_far) + len(after)
+    scratch = []
+    for _, many, _ in groups:
+        scratch.append(pltpu.VMEM((tokens, many * size), BF16))
+        scratch.append(pltpu.VMEM((many, size, size), F32))
     return pl.pallas_call(
-        functools.partial(final_kernel, first, heads, kind, unread),
-        in_specs=[pl.BlockSpec(memory_space=pltpu.SMEM)] + [vmem] * 8 + [anywhere] * unread,
+        functools.partial(final_kernel, groups, unread),
+        in_specs=[pl.BlockSpec(memory_space=pltpu.SMEM)]
+        + [vmem] * (2 + len(arrays))
+        + [anywhere] * unread,
         out_specs=[anywhere, anywhere],
         out_shape=[
             jax.ShapeDtypeStruct((tokens, total * size), BF16),
             jax.ShapeDtypeStruct((1, total, size, size), F32),
         ],
-        scratch_shapes=[
-            pltpu.VMEM((tokens, heads * size), BF16),
-            pltpu.VMEM((heads, size, size), F32),
-            pltpu.SemaphoreType.DMA((2 * heads,)),
-        ],
-        input_output_aliases={9 + i: i for i in range(len(so_far))},
-        compiler_params=pltpu.CompilerParams(vmem_limit_bytes=8 * MIB),
+        scratch_shapes=scratch + [pltpu.SemaphoreType.DMA((2 * total,))],
+        input_output_aliases={3 + len(arrays) + i: i for i in range(len(so_far))},
+        compiler_params=pltpu.CompilerParams(vmem_limit_bytes=12 * MIB),
         cost_estimate=SHORT,
         name="finish",
-    )(order, seg, own, near, past, o, gate, q, a, *so_far, *after)
+    )(order, seg, a, *arrays, *so_far, *after)
 
 
 def shards(q, k, v, g, segment, decay_exponent, retention, norm_gain):
@@ -426,22 +422,26 @@
         )
         return copied
 
+    def pair_first(i, after):
+        both = joined(order, own[i], near[i], chunks[i][1], after)
+        past[i] = turn(both)
+        return both
+
+    def pair_last(i, after):
+        message = picked(order, own[i], past[i], after)
+        near[i] = swap(message)
+        return message
+
     own[2], own[3] = look_inside(0, (own[2], own[3]))
+    near[3] = swap(own[3])
+    first_done = pair_first(1, (own[2],))
     past[2] = turn(own[2])
-    near[3] = swap(own[3])
-    look_inside(1, (), (own[2], own[3]))
-
-    def second_hops(i, after):
-        picks = picked(order, own[i], past[i], after)
-        near[i] = swap(picks)
-        both = joined(order, own[i + 1], near[i + 1], chunks[i + 1][1], (picks,))
-        past[i + 1] = turn(both)
-        return both
-
-    both = second_hops(0, (inside[1][0],))
-    look_inside(2, (), (both,))
-    look_inside(3, (), (both,))
-    both = second_hops(2, (inside[2][0], inside[3][0]))
+    second_done = pair_last(0, (first_done,))
+    look_inside(1, (), (second_done,))
+    look_inside(2, (), (inside[1][0],))
+    look_inside(3, (), (inside[2][0],))
+    second_done = pair_last(2, (inside[3][0],))
+    first_done = pair_first(3, (second_done,))
 
     if reach > 2:
         for i, (_, many) in enumerate(chunks):
@@ -454,11 +454,10 @@
                 past[i] = widened(jnp.where(place >= 2, past[i], 0.0), many, 2, 2)
 
     result = ()
-    for i, (first, many) in enumerate(chunks):
-        result = finish(
-            order, seg, own[i], near[i], past[i], *inside[i], a, result, (both,), first, many,
-            ("span", "pair")[i % 2],
-        )
+    for group in ((0, 1), (2, 3)):
+        groups = [(*chunks[i], ("span", "pair")[i % 2]) for i in group]
+        arrays = [x for i in group for x in (own[i], near[i], past[i], *inside[i])]
+        result = finish(order, seg, a, groups, arrays, result, (first_done,))
     return tuple(result)
 
 

time: 35.3 us -> 36.5 us (1.034)
  waiting for transfers between devices: 4.48 us -> 8.42 us
  starting transfers between devices: 12.1 us -> 10.1 us
  Pallas kernels: 17.8 us -> 17 us
    ppermute x4, waiting for transfers between devices: 0.01 us -> 5.4 us  [shards(): lax.ppermute(x, 'seq', [(c, (c + 2) % count) for c in range(count)])]
    ppermute x4, starting transfers between devices: 7.38 us -> 4.44 us  [shards(): lax.ppermute(x, 'seq', [(c, (c + 2) % count) for c in range(count)])]
    ppermute x4, waiting for transfers between devices: 4.47 us -> 3.02 us  [shards(): swap = lambda x: lax.ppermute(x, 'seq', [(c, c ^ 1) for c in range(count)])]
    ppermute x4, starting transfers between devices: 4.75 us -> 5.69 us  [shards(): swap = lambda x: lax.ppermute(x, 'seq', [(c, c ^ 1) for c in range(count)])]
    pallas_call x4 -> x2, Pallas kernels: 6.57 us -> 5.76 us  [finish(): pl.pallas_call(functools.partial(final_kernel, groups, unread), in_specs=...]
  transfers between devices with their start and end apart: 8 -> 8, of which waited for: 1 -> 3; matrix products, arithmetic and copies ran while one was open for 0% -> 0% of each run, Pallas kernels for 40% -> 34%
where the time goes in v2:
time: 36.5 us; the launch traced here: 36.3 us
  Pallas kernels  17 us (47%)
  starting transfers between devices  10.1 us (28%)
  waiting for transfers between devices  8.42 us (23%)
  between operations  0.74 us (2%)
    pallas_call x4, Pallas kernels, intra(): pl.pallas_call(functools.partial(intra_kernel, first, heads, len(through)...  6.1 us
    pallas_call x2, Pallas kernels, finish(): pl.pallas_call(functools.partial(final_kernel, groups, unread), in_specs=...  5.76 us
    ppermute x4, starting transfers between devices, shards(): swap = lambda x: lax.ppermute(x, 'seq', [(c, c ^ 1) for c in range(count)])  5.69 us
    ppermute x4, waiting for transfers between devices, shards(): lax.ppermute(x, 'seq', [(c, (c + 2) % count) for c in range(count)])  5.4 us
    ppermute x4, starting transfers between devices, shards(): lax.ppermute(x, 'seq', [(c, (c + 2) % count) for c in range(count)])  4.44 us
    ppermute x4, waiting for transfers between devices, shards(): swap = lambda x: lax.ppermute(x, 'seq', [(c, c ^ 1) for c in range(count)])  3.02 us
    pallas_call x1, Pallas kernels, rest_messages(): pl.pallas_call(functools.partial(rest_kernel, chunks, done), in_specs=[pl...  2.81 us
    pallas_call x1, Pallas kernels, first_messages(): pl.pallas_call(functools.partial(first_kernel, heads, chunks), in_specs=[...  2.21 us
  transfers between devices with their start and end apart: 8, of which 3 were waited for; matrix products, arithmetic and copies ran while one was open for 0% of the time, Pallas kernels for 34%

profile of v2, /device:TPU:0, one launch (start us, length us, event | category | flops | bytes accessed | tf_op | source)
XLA Modules:
  0.0 36.3 jit_solution(16011607047291932495)
XLA Ops:
  0.6 2.2 %first_messages.1 = (f32[648,128]{1,0:T(8,128)S(1)}, f32[648,128]{1,0:T(8,128)S(1)}, f32[16,512]{1,0:T(8,128)S(1)}, f32[16,512]{1,0:T(8,128)S(1)}, s32[1,512]{1,...) custom-call(s32[1]{0:T(128)} %bitcast.order_ref, ...), custom_call_target="tpu_custom_call" | custom-call | flops 1 | bytes 1 | tf_op jit(solution)/shard_map/first_messages/pallas_call | solution.py:99
  2.9 3.0 %collective-permute-start.2 = (f32[648,128]{1,0:T(8,128)S(1)}, f32[648,128]{1,0:T(8,128)S(1)}, u32[]{:S(2)}, u32[]{:S(2)}) collective-permute-start(f32[648,128]{1,0:T(8,128)S(1)} %get-tuple-element.62.first_ref.rest_6_), channel_id=1, source_target_pairs={{0,2},{2,0},{4,6},{6,4},{8,10},{10,8},{12,14},{14,12},{1,3},{3,1},... | collective-permute-start | bytes 995336 | tf_op jit(solution)/shard_map/ppermute | solution.py:386
  5.9 1.6 %collective-permute-start.1 = (f32[648,128]{1,0:T(8,128)S(1)}, f32[648,128]{1,0:T(8,128)S(1)}, u32[]{:S(2)}, u32[]{:S(2)}) collective-permute-start(f32[648,128]{1,0:T(8,128)S(1)} %get-tuple-element.61.first_ref.rest_0_), channel_id=1, source_target_pairs={{0,4},{2,6},{4,8},{6,10},{8,12},{10,14},{12,0},{14,2},{1,5},{3,7},... | collective-permute-start | bytes 995336 | tf_op jit(solution)/shard_map/ppermute | solution.py:387
  7.4 2.8 %rest_messages.1 = (f32[392,128]{1,0:T(8,128)S(1)}, f32[392,128]{1,0:T(8,128)S(1)}, f32[512,512]{1,0:T(8,128)S(1)}, bf16[512,384]{1,0:T(8,128)(2,1)S(1)}, bf16[5...) custom-call(s32[1,512]{1,0:T(1,128)S(1)} %get-tuple-element.38.seg_r, ...), custom_call_target="tpu_custom_call" | custom-call | flops 1 | bytes 1 | tf_op jit(solution)/shard_map/rest_messages/pallas_call | solution.py:154
  10.3 1.8 %intra_span.4 = (f32[512,640]{1,0:T(8,128)S(1)}, f32[512,640]{1,0:T(8,128)S(1)}, f32[392,128]{1,0:T(8,128)S(1)}, f32[392,128]{1,0:T(8,128)S(1)}) custom-call(f32[512,512]{1,0:T(8,128)S(1)} %get-tuple-element.41.mask_ref, f32[16,512]{1,0:T(8,128)S(1)} %get-tuple-element.39.a_ref, f32[1,2048]{1,0:T(1,128)S(1)} %bitcast.4, ...), custom_call_target="tpu_custom_call" | custom-call | flops 1 | bytes 1 | tf_op jit(solution)/shard_map/intra_span/pallas_call | solution.py:269
  12.1 1.6 %collective-permute-start = (f32[392,128]{1,0:T(8,128)S(1)}, f32[392,128]{1,0:T(8,128)S(1)}, u32[]{:S(2)}, u32[]{:S(2)}) collective-permute-start(f32[392,128]{1,0:T(8,128)S(1)} %get-tuple-element.48.rest_0_.first_ref), channel_id=1, source_target_pairs={{0,4},{2,6},{4,8},{6,10},{8,12},{10,14},{12,0},{14,2},{1,5},{3,7},... | collective-permute-start | bytes 602120 | tf_op jit(solution)/shard_map/ppermute | solution.py:387
  13.7 0.5 %collective-permute-start.4 = (f32[392,128]{1,0:T(8,128)S(1)}, f32[392,128]{1,0:T(8,128)S(1)}, u32[]{:S(2)}, u32[]{:S(2)}) collective-permute-start(f32[392,128]{1,0:T(8,128)S(1)} %get-tuple-element.67.first_ref.rest_6_), channel_id=1, source_target_pairs={{0,2},{2,0},{4,6},{6,4},{8,10},{10,8},{12,14},{14,12},{1,3},{3,1},... | collective-permute-start | bytes 602120 | tf_op jit(solution)/shard_map/ppermute | solution.py:386
  14.3 0.0 collective-permute-done.2.second_ref.rest_7_
  14.3 0.1 join_windows.2.rest_0_
  14.3 3.7 %collective-permute-done.1.second_ref.rest_2_ = f32[648,128]{1,0:T(8,128)S(1)} collective-permute-done((f32[648,128]{1,0:T(8,128)S(1)}, f32[648,128]{1,0:T(8,128)S(1)}, u32[]{:S(2)}, u32[]{:S(2)}) %collective-permute-start.1) | collective-permute-done | bytes 331808 | tf_op jit(solution)/shard_map/ppermute | solution.py:387
  18.1 0.7 %collective-permute-start.6 = (f32[648,128]{1,0:T(8,128)S(1)}, f32[648,128]{1,0:T(8,128)S(1)}, u32[]{:S(2)}, u32[]{:S(2)}) collective-permute-start(f32[648,128]{1,0:T(8,128)S(1)} %pick_message.2.refs_0_), channel_id=1, source_target_pairs={{0,2},{2,0},{4,6},{6,4},{8,10},{10,8},{12,14},{14,12},{1,3},{3,1},... | collective-permute-start | bytes 995336 | tf_op jit(solution)/shard_map/ppermute | solution.py:386
  18.8 0.0 collective-permute-start.7
  18.8 1.8 %intra_span.5 = (f32[512,640]{1,0:T(8,128)S(1)}, f32[512,640]{1,0:T(8,128)S(1)}) custom-call(f32[512,512]{1,0:T(8,128)S(1)} %get-tuple-element.41.mask_ref, f32[16,512]{1,0:T(8,128)S(1)} %get-tuple-element.39.a_ref, f32[1,2048]{1,0:T(1,128)S(1)} %bitcast.5, bf16[512,640]{1,0:T(8,128)(2,1)S(1)} %get-tuple-element.57.q_ref.rest_11_, ...), custom_call_target="tpu_custom_call" | custom-call | flops 1 | bytes 1 | tf_op jit(solution)/shard_map/intra_span/pallas_call | solution.py:269
  20.6 1.2 %intra_span.6 = (f32[512,384]{1,0:T(8,128)S(1)}, f32[512,384]{1,0:T(8,128)S(1)}) custom-call(f32[512,512]{1,0:T(8,128)S(1)} %get-tuple-element.41.mask_ref, f32[16,512]{1,0:T(8,128)S(1)} %get-tuple-element.39.a_ref, f32[1,2048]{1,0:T(1,128)S(1)} %bitcast.6, bf16[512,384]{1,0:T(8,128)(2,1)S(1)} %get-tuple-element.53.q_ref.rest_5_, ...), custom_call_target="tpu_custom_call" | custom-call | flops 1 | bytes 1 | tf_op jit(solution)/shard_map/intra_span/pallas_call | solution.py:269
  21.8 1.2 %intra_span.7 = (f32[512,384]{1,0:T(8,128)S(1)}, f32[512,384]{1,0:T(8,128)S(1)}) custom-call(f32[512,512]{1,0:T(8,128)S(1)} %get-tuple-element.41.mask_ref, f32[16,512]{1,0:T(8,128)S(1)} %get-tuple-element.39.a_ref, f32[1,2048]{1,0:T(1,128)S(1)} %bitcast.7, bf16[512,384]{1,0:T(8,128)(2,1)S(1)} %get-tuple-element.49.q_ref.rest_11_, ...), custom_call_target="tpu_custom_call" | custom-call | flops 1 | bytes 1 | tf_op jit(solution)/shard_map/intra_span/pallas_call | solution.py:269
  23.0 0.0 collective-permute-done.second_ref.rest_2_
  23.1 0.0 collective-permute-done.4.second_ref.rest_7_
  23.1 1.2 %collective-permute-start.5 = (f32[392,128]{1,0:T(8,128)S(1)}, f32[392,128]{1,0:T(8,128)S(1)}, u32[]{:S(2)}, u32[]{:S(2)}) collective-permute-start(f32[392,128]{1,0:T(8,128)S(1)} %join_windows.3.rest_12_.rest_14_), channel_id=1, source_target_pairs={{0,4},{2,6},{4,8},{6,10},{8,12},{10,14},{12,0},{14,2},{1,5},{3,7},... | collective-permute-start | bytes 602120 | tf_op jit(solution)/shard_map/ppermute | solution.py:387
  24.4 1.5 %collective-permute-start.3 = (f32[392,128]{1,0:T(8,128)S(1)}, f32[392,128]{1,0:T(8,128)S(1)}, u32[]{:S(2)}, u32[]{:S(2)}) collective-permute-start(f32[392,128]{1,0:T(8,128)S(1)} %pick_message.3.rest_0_), channel_id=1, source_target_pairs={{0,2},{2,0},{4,6},{6,4},{8,10},{10,8},{12,14},{14,12},{1,3},{3,1},... | collective-permute-start | bytes 602120 | tf_op jit(solution)/shard_map/ppermute | solution.py:386
  25.9 3.0 %collective-permute-done.6.rest_1_ = f32[648,128]{1,0:T(8,128)S(1)} collective-permute-done((f32[648,128]{1,0:T(8,128)S(1)}, f32[648,128]{1,0:T(8,128)S(1)}, u32[]{:S(2)}, u32[]{:S(2)}) %collective-permute-start.6) | collective-permute-done | bytes 331808 | tf_op jit(solution)/shard_map/ppermute | solution.py:386
  28.9 1.7 %collective-permute-done.7.rest_8_ = f32[648,128]{1,0:T(8,128)S(1)} collective-permute-done((f32[648,128]{1,0:T(8,128)S(1)}, f32[648,128]{1,0:T(8,128)S(1)}, u32[]{:S(2)}, u32[]{:S(2)}) %collective-permute-start.7) | collective-permute-done | bytes 331808 | tf_op jit(solution)/shard_map/ppermute | solution.py:387
  30.5 3.3 %finish.2 = (bf16[512,2048]{1,0:T(8,128)(2,1)}, f32[1,16,128,128]{3,2,1,0:T(8,128)}) custom-call(s32[1]{0:T(128)} %bitcast.order_ref, s32[1,512]{1,0:T(1,128)S(1)} %get-tuple-element.38.seg_ref, f32[16,512]{1,0:T(8,128)S(1)} %get-tuple-element.39.a_ref, f32[648,128]{1,0:T(8,128)S(1)} %get-tuple-element.61.first_ref.rest_0_, ...), custom_call_target="tpu_custom_call" | custom-call | flops 1 | bytes 1 | tf_op jit(solution)/shard_map/finish/pallas_call | solution.py:357
  33.8 0.0 collective-permute-done.3.rest_1_
  33.9 2.5 %finish.3 = (bf16[512,2048]{1,0:T(8,128)(2,1)}, f32[1,16,128,128]{3,2,1,0:T(8,128)}) custom-call(s32[1]{0:T(128)} %bitcast.order_ref, s32[1,512]{1,0:T(1,128)S(1)} %get-tuple-element.38.seg_ref, f32[16,512]{1,0:T(8,128)S(1)} %get-tuple-element.39.a_ref, ...), custom_call_target="tpu_custom_call", output_to_operand_aliasing={{0}: (15, {}), {1}: (16, {})} | custom-call | flops 1 | bytes 1 | tf_op jit(solution)/shard_map/finish/pallas_call | solution.py:357
  (6 shorter events, 0.1 us)
Async XLA Ops:
  2.9 11.4 %collective-permute-start.2 = (f32[648,128]{1,0:T(8,128)S(1)}, f32[648,128]{1,0:T(8,128)S(1)}, u32[]{:S(2)}, u32[]{:S(2)}) collective-permute-start(f32[648,128]{1,0:T(8,128)S(1)} %get-tuple-element.62.first_ref.rest_6_), channel_id=1, source_target_pairs={{0,2},{2,0},{4,6},{6,4},{8,10},{10,8},{12,14},{14,12},{1,3},{3,1},... | collective-permute-start | bytes 995336 | tf_op jit(solution)/shard_map/ppermute | solution.py:386
  5.9 12.2 %collective-permute-start.1 = (f32[648,128]{1,0:T(8,128)S(1)}, f32[648,128]{1,0:T(8,128)S(1)}, u32[]{:S(2)}, u32[]{:S(2)}) collective-permute-start(f32[648,128]{1,0:T(8,128)S(1)} %get-tuple-element.61.first_ref.rest_0_), channel_id=1, source_target_pairs={{0,4},{2,6},{4,8},{6,10},{8,12},{10,14},{12,0},{14,2},{1,5},{3,7},... | collective-permute-start | bytes 995336 | tf_op jit(solution)/shard_map/ppermute | solution.py:387
  7.4 2.8 %copy-start = (f32[2048]{0:T(1024)S(1)}, f32[2048]{0:T(1024)}, u32[]{:S(2)}) copy-start(f32[2048]{0:T(1024)} %param.15) | copy-start | bytes 24580
  12.1 10.9 %collective-permute-start = (f32[392,128]{1,0:T(8,128)S(1)}, f32[392,128]{1,0:T(8,128)S(1)}, u32[]{:S(2)}, u32[]{:S(2)}) collective-permute-start(f32[392,128]{1,0:T(8,128)S(1)} %get-tuple-element.48.rest_0_.first_ref), channel_id=1, source_target_pairs={{0,4},{2,6},{4,8},{6,10},{8,12},{10,14},{12,0},{14,2},{1,5},{3,7},... | collective-permute-start | bytes 602120 | tf_op jit(solution)/shard_map/ppermute | solution.py:387
  13.7 9.4 %collective-permute-start.4 = (f32[392,128]{1,0:T(8,128)S(1)}, f32[392,128]{1,0:T(8,128)S(1)}, u32[]{:S(2)}, u32[]{:S(2)}) collective-permute-start(f32[392,128]{1,0:T(8,128)S(1)} %get-tuple-element.67.first_ref.rest_6_), channel_id=1, source_target_pairs={{0,2},{2,0},{4,6},{6,4},{8,10},{10,8},{12,14},{14,12},{1,3},{3,1},... | collective-permute-start | bytes 602120 | tf_op jit(solution)/shard_map/ppermute | solution.py:386
  18.1 10.8 %collective-permute-start.6 = (f32[648,128]{1,0:T(8,128)S(1)}, f32[648,128]{1,0:T(8,128)S(1)}, u32[]{:S(2)}, u32[]{:S(2)}) collective-permute-start(f32[648,128]{1,0:T(8,128)S(1)} %pick_message.2.refs_0_), channel_id=1, source_target_pairs={{0,2},{2,0},{4,6},{6,4},{8,10},{10,8},{12,14},{14,12},{1,3},{3,1},... | collective-permute-start | bytes 995336 | tf_op jit(solution)/shard_map/ppermute | solution.py:386
  18.8 11.8 %collective-permute-start.7 = (f32[648,128]{1,0:T(8,128)S(1)}, f32[648,128]{1,0:T(8,128)S(1)}, u32[]{:S(2)}, u32[]{:S(2)}) collective-permute-start(f32[648,128]{1,0:T(8,128)S(1)} %join_windows.2.rest_0_), channel_id=1, source_target_pairs={{0,4},{2,6},{4,8},{6,10},{8,12},{10,14},{12,0},{14,2},{1,5},{3,7},... | collective-permute-start | bytes 995336 | tf_op jit(solution)/shard_map/ppermute | solution.py:387
  23.1 10.7 %collective-permute-start.5 = (f32[392,128]{1,0:T(8,128)S(1)}, f32[392,128]{1,0:T(8,128)S(1)}, u32[]{:S(2)}, u32[]{:S(2)}) collective-permute-start(f32[392,128]{1,0:T(8,128)S(1)} %join_windows.3.rest_12_.rest_14_), channel_id=1, source_target_pairs={{0,4},{2,6},{4,8},{6,10},{8,12},{10,14},{12,0},{14,2},{1,5},{3,7},... | collective-permute-start | bytes 602120 | tf_op jit(solution)/shard_map/ppermute | solution.py:387
  24.4 9.5 %collective-permute-start.3 = (f32[392,128]{1,0:T(8,128)S(1)}, f32[392,128]{1,0:T(8,128)S(1)}, u32[]{:S(2)}, u32[]{:S(2)}) collective-permute-start(f32[392,128]{1,0:T(8,128)S(1)} %pick_message.3.rest_0_), channel_id=1, source_target_pairs={{0,2},{2,0},{4,6},{6,4},{8,10},{10,8},{12,14},{14,12},{1,3},{3,1},... | collective-permute-start | bytes 602120 | tf_op jit(solution)/shard_map/ppermute | solution.py:386
